TPU v7x, 32 devices: a whole 2x2x4 slice. The times are simulated.
32 devices in a mesh: section: 2 (over x), dp: 4 (over z), mp: 4 (over y, core).
Axes of the slice: x: 2, y: 2, z: 4, core: 2. Of those that a mesh axis runs over, the one named last changes fastest.
Arguments:
- x_visible: bfloat16 [8, 512, 768], P('dp', 'mp'), may hold values from -6 to 6
- resolution: int32 [8], P('dp'), may hold values from 0 to 1, as said below
- visible_index: int32 [8, 512], P('dp'), may hold values from 0 to 2047, as said below
- enc_qkv_w: bfloat16 [768, 3, 768], P(('section', 'dp'), None, 'mp'), may hold values from -0.21875 to 0.21875
- enc_out_w: bfloat16 [768, 768], P('mp', ('section', 'dp')), may hold values from -0.875 to 0.875
- enc_up_w: bfloat16 [768, 3072], P(('section', 'dp'), 'mp'), may hold values from -0.21875 to 0.21875
- enc_down_w: bfloat16 [3072, 768], P('mp', ('section', 'dp')), may hold values from -0.109375 to 0.109375
- enc_gains: float32 [2, 768], replicated, may hold values from 0.1 to 1.9
- enc_shifts: float32 [2, 768], replicated, may hold values from -1.8 to 1.8
- projection: bfloat16 [768, 512], replicated, may hold values from -0.21875 to 0.21875
- mask_token: float32 [512], replicated, may hold values from -5 to 5
- dec_qkv_w: bfloat16 [512, 3, 512], P(('section', 'dp'), None, 'mp'), may hold values from -0.25 to 0.25
- dec_out_w: bfloat16 [512, 512], P('mp', ('section', 'dp')), may hold values from -1.5 to 1.5
- dec_up_w: bfloat16 [512, 2048], P(('section', 'dp'), 'mp'), may hold values from -0.25 to 0.25
- dec_down_w: bfloat16 [2048, 512], P('mp', ('section', 'dp')), may hold values from -0.125 to 0.125
- dec_gains: float32 [2, 512], replicated, may hold values from 0.1 to 1.9
- dec_shifts: float32 [2, 512], replicated, may hold values from -1.8 to 1.8
- cotangent: bfloat16 [8, 2048, 512], P('dp', 'mp'), may hold values from -6 to 6
Outputs:
- decoded: bfloat16 [8, 2048, 512], P('dp', 'mp', 'section')
- input_grad: float32 [8, 512, 768], P('dp', 'mp', 'section')
- enc_qkv_grad: float32 [768, 3, 768], P(('section', 'dp'), None, 'mp')
- enc_out_grad: float32 [768, 768], P('mp', ('section', 'dp'))
- enc_up_grad: float32 [768, 3072], P(('section', 'dp'), 'mp')
- enc_down_grad: float32 [3072, 768], P('mp', ('section', 'dp'))
- enc_gains_grad: float32 [2, 768], replicated
- enc_shifts_grad: float32 [2, 768], replicated
- projection_grad: float32 [768, 512], replicated
- mask_grad: float32 [512], replicated
- dec_qkv_grad: float32 [512, 3, 512], P(('section', 'dp'), None, 'mp')
- dec_out_grad: float32 [512, 512], P('mp', ('section', 'dp'))
- dec_up_grad: float32 [512, 2048], P(('section', 'dp'), 'mp')
- dec_down_grad: float32 [2048, 512], P('mp', ('section', 'dp'))
- dec_gains_grad: float32 [2, 512], replicated
- dec_shifts_grad: float32 [2, 512], replicated
Inputs may be any that keep to these rules, and one draw needn't show every extreme that they name: `resolution`: 1 selects the 32 x 64 grid, 0 the 16 x 32 grid; samples 2k and 2k + 1 hold at least one 1 for each k. `visible_index`: for a big-grid sample the 512 entries are distinct positions below 2048; for a small-grid sample the first 128 entries are distinct positions below 512 and the others are 0. Position p lies in row p // width and column p % width of its grid.
All inputs are finite; a program needn't handle non-finite values.
Results may differ from a plain program's by a relative error of at most 0.018.
Values may be sent and summed in bfloat16 or wider, within the bound.
A program may use at most 256 MiB of HBM per device.

v0:
```python
import jax
import jax.numpy as jnp
from jax import lax
from jax.sharding import PartitionSpec as P

HD_ENC = 64
HD_DEC = 32
COLS_SMALL = 32
COLS_BIG = 64
PATCHES = 2048
SMALL_PATCHES = 512
VIS = 512
VIS_SMALL = 128


def shifted(value, axis, steps):
    count = lax.axis_size(axis)
    leading, last = (max(0, -steps), min(count, count - steps))
    return lax.ppermute(value, axis, [(source, source + steps) for source in range(leading, last)])


def normalize(stream, gain_row, shift_row):
    centre = stream - jnp.mean(stream, axis=-1, keepdims=True)
    inverse = lax.rsqrt(jnp.mean(centre * centre, axis=-1, keepdims=True) + 1e-06)
    return centre * inverse * gain_row + shift_row


def normalize_back(stream, gain_row, grad_out):
    centre = stream - jnp.mean(stream, axis=-1, keepdims=True)
    inverse = lax.rsqrt(jnp.mean(centre * centre, axis=-1, keepdims=True) + 1e-06)
    scaled = centre * inverse
    grad_scaled = grad_out * gain_row
    grad_in = inverse * (
        grad_scaled
        - jnp.mean(grad_scaled, axis=-1, keepdims=True)
        - scaled * jnp.mean(grad_scaled * scaled, axis=-1, keepdims=True)
    )
    return (grad_in, jnp.sum(grad_out * scaled, axis=0), jnp.sum(grad_out, axis=0))


def sincos_table(positions, grid_width, model_width):
    quarter = model_width // 4
    frequency = 10000.0 ** (-jnp.arange(quarter, dtype=jnp.float32) / quarter)
    rows_at = (positions // grid_width).astype(jnp.float32)
    cols_at = (positions % grid_width).astype(jnp.float32)
    row_angle = rows_at[:, None] * frequency[None, :]
    col_angle = cols_at[:, None] * frequency[None, :]
    return jnp.concatenate(
        [jnp.sin(row_angle), jnp.cos(row_angle), jnp.sin(col_angle), jnp.cos(col_angle)], axis=-1
    )


def gelu_exact(values):
    return jax.nn.gelu(values, approximate=False)


def collect(rows_low):
    return lax.all_gather(rows_low, "mp", axis=0, tiled=True)


def spread(left_rows, weight):
    return lax.psum_scatter(
        jnp.dot(left_rows, weight, preferred_element_type=jnp.float32),
        "mp",
        scatter_dimension=0,
        tiled=True,
    )


def attend(qkv_rows, key_live, head_dim):
    length = qkv_rows.shape[0]
    local_width = qkv_rows.shape[2]
    head_count = local_width // head_dim
    split_rows = qkv_rows.reshape(length, 3, head_count, head_dim)
    queries = split_rows[:, 0]
    key_rows = split_rows[:, 1]
    value_rows = split_rows[:, 2]
    block_rows = min(512, length)
    score_scale = head_dim ** (-0.5)

    def one_block(row_start):
        query_block = lax.dynamic_slice_in_dim(queries, row_start, block_rows, 0)
        raw_scores = jnp.einsum(
            "qhd,khd->hqk", query_block, key_rows, preferred_element_type=jnp.float32
        )
        scores = jnp.where(key_live[None, None, :], raw_scores * score_scale, -1e30)
        top_score = jnp.max(scores, axis=-1, keepdims=True)
        weights = jnp.exp(scores - top_score)
        totals = jnp.sum(weights, axis=-1, keepdims=True)
        prob_low = (weights / totals).astype(jnp.bfloat16)
        context = jnp.einsum(
            "hqk,khd->qhd", prob_low, value_rows, preferred_element_type=jnp.float32
        )
        return (
            context.astype(jnp.bfloat16).reshape(block_rows, local_width),
            (top_score + jnp.log(totals))[:, :, 0],
        )

    def block_step(row_start):
        return one_block(row_start)

    contexts, log_totals = lax.map(block_step, jnp.arange(length // block_rows) * block_rows)
    return (
        contexts.reshape(length, local_width),
        jnp.transpose(log_totals, (1, 0, 2)).reshape(head_count, length),
    )


def attend_back(qkv_rows, log_totals, grad_context, key_live, head_dim):
    length = qkv_rows.shape[0]
    local_width = qkv_rows.shape[2]
    head_count = local_width // head_dim
    split_rows = qkv_rows.reshape(length, 3, head_count, head_dim)
    queries = split_rows[:, 0]
    key_rows = split_rows[:, 1]
    value_rows = split_rows[:, 2]
    grad_heads = grad_context.reshape(length, head_count, head_dim)
    block_rows = min(512, length)
    score_scale = head_dim ** (-0.5)

    def one_block(running, row_start):
        grad_keys, grad_values = running
        query_block = lax.dynamic_slice_in_dim(queries, row_start, block_rows, 0)
        grad_block = lax.dynamic_slice_in_dim(grad_heads, row_start, block_rows, 0)
        log_block = lax.dynamic_slice_in_dim(log_totals, row_start, block_rows, 1)
        raw_scores = jnp.einsum(
            "qhd,khd->hqk", query_block, key_rows, preferred_element_type=jnp.float32
        )
        scores = jnp.where(key_live[None, None, :], raw_scores * score_scale, -1e30)
        weights = jnp.exp(scores - log_block[:, :, None])
        grad_weights = jnp.einsum(
            "qhd,khd->hqk", grad_block, value_rows, preferred_element_type=jnp.float32
        )
        grad_scores = weights * (
            grad_weights - jnp.sum(weights * grad_weights, axis=-1, keepdims=True)
        )
        grad_raw = (grad_scores * score_scale).astype(jnp.bfloat16)
        grad_query = jnp.einsum(
            "hqk,khd->qhd", grad_raw, key_rows, preferred_element_type=jnp.float32
        )
        grad_keys = grad_keys + jnp.einsum(
            "hqk,qhd->khd", grad_raw, query_block, preferred_element_type=jnp.float32
        )
        grad_values = grad_values + jnp.einsum(
            "hqk,qhd->khd",
            weights.astype(jnp.bfloat16),
            grad_block,
            preferred_element_type=jnp.float32,
        )
        return ((grad_keys, grad_values), grad_query.astype(jnp.bfloat16))

    def block_step(running, row_start):
        return one_block(running, row_start)

    empty_sum = jnp.zeros((length, head_count, head_dim), jnp.float32)
    (grad_keys, grad_values), grad_queries = lax.scan(
        block_step, (empty_sum, empty_sum), jnp.arange(length // block_rows) * block_rows
    )
    stacked = jnp.stack(
        [
            grad_queries.reshape(length, head_count, head_dim),
            grad_keys.astype(jnp.bfloat16),
            grad_values.astype(jnp.bfloat16),
        ],
        axis=1,
    )
    return stacked.reshape(length, 3, local_width)


def block_forward(stream, matrices, gain_rows, shifts, key_live, head_dim):
    qkv_weight, out_weight, up_weight, down_weight = matrices
    normed = normalize(stream, gain_rows[0], shifts[0]).astype(jnp.bfloat16)
    normed_all = collect(normed)
    qkv_rows = jnp.einsum(
        "ld,dtc->ltc", normed_all, qkv_weight, preferred_element_type=jnp.float32
    ).astype(jnp.bfloat16)
    context, log_totals = attend(qkv_rows, key_live, head_dim)
    middle = stream + spread(context, out_weight)
    normed_mid = normalize(middle, gain_rows[1], shifts[1]).astype(jnp.bfloat16)
    normed_mid_all = collect(normed_mid)
    hidden = jnp.dot(normed_mid_all, up_weight, preferred_element_type=jnp.float32)
    active = gelu_exact(hidden).astype(jnp.bfloat16)
    result = middle + spread(active, down_weight)
    return (
        result,
        (stream, middle, normed_all, normed_mid_all, qkv_rows, context, log_totals, hidden, active),
    )


def block_backward(grad_out, saved_state, matrices, gain_rows, key_live, head_dim):
    qkv_weight, out_weight, up_weight, down_weight = matrices
    stream, middle, normed_all, normed_mid_all, qkv_rows, context, log_totals, hidden, active = (
        saved_state
    )
    length = qkv_rows.shape[0]
    grad_branch = collect(grad_out.astype(jnp.bfloat16))
    down_grad = jnp.dot(active.T, grad_branch, preferred_element_type=jnp.float32)
    grad_active = jnp.dot(grad_branch, down_weight.T, preferred_element_type=jnp.float32)
    grad_hidden = jax.vjp(gelu_exact, hidden)[1](grad_active)[0].astype(jnp.bfloat16)
    up_grad = jnp.dot(normed_mid_all.T, grad_hidden, preferred_element_type=jnp.float32)
    grad_norm_mid = spread(grad_hidden, up_weight.T)
    back_mid, gain_mid, shift_mid = normalize_back(middle, gain_rows[1], grad_norm_mid)
    grad_middle = grad_out + back_mid
    grad_attended = collect(grad_middle.astype(jnp.bfloat16))
    out_grad = jnp.dot(context.T, grad_attended, preferred_element_type=jnp.float32)
    grad_context = jnp.dot(grad_attended, out_weight.T, preferred_element_type=jnp.float32).astype(
        jnp.bfloat16
    )
    grad_qkv = attend_back(qkv_rows, log_totals, grad_context, key_live, head_dim)
    qkv_grad = jnp.einsum("ld,ltc->dtc", normed_all, grad_qkv, preferred_element_type=jnp.float32)
    grad_normed = spread(
        grad_qkv.reshape(length, -1), qkv_weight.reshape(qkv_weight.shape[0], -1).T
    )
    back_in, gain_in, shift_in = normalize_back(stream, gain_rows[0], grad_normed)
    return (
        grad_middle + back_in,
        (
            qkv_grad,
            out_grad,
            up_grad,
            down_grad,
            jnp.stack([gain_in, gain_mid]),
            jnp.stack([shift_in, shift_mid]),
        ),
    )


def per_device(
    x_visible,
    resolution,
    visible_index,
    enc_qkv_w,
    enc_out_w,
    enc_up_w,
    enc_down_w,
    enc_gains,
    enc_shifts,
    projection,
    mask_token,
    dec_qkv_w,
    dec_out_w,
    dec_up_w,
    dec_down_w,
    dec_gains,
    dec_shifts,
    cotangent,
):
    gathered = (
        lax.all_gather(enc_qkv_w, ("section", "dp"), axis=0, tiled=True),
        lax.all_gather(enc_out_w, ("section", "dp"), axis=1, tiled=True),
        lax.all_gather(enc_up_w, ("section", "dp"), axis=0, tiled=True),
        lax.all_gather(enc_down_w, ("section", "dp"), axis=1, tiled=True),
        lax.all_gather(dec_qkv_w, ("section", "dp"), axis=0, tiled=True),
        lax.all_gather(dec_out_w, ("section", "dp"), axis=1, tiled=True),
        lax.all_gather(dec_up_w, ("section", "dp"), axis=0, tiled=True),
        lax.all_gather(dec_down_w, ("section", "dp"), axis=1, tiled=True),
    )
    enc_mats = (gathered[0], gathered[1], gathered[2], gathered[3])
    dec_mats = (gathered[4], gathered[5], gathered[6], gathered[7])
    micro_count = x_visible.shape[0]
    enc_rows = x_visible.shape[1]
    enc_width = x_visible.shape[2]
    dec_rows = cotangent.shape[1]
    dec_width = cotangent.shape[2]
    vis_total = visible_index.shape[1]
    grid_total = dec_rows * lax.axis_size("mp")
    section_first = lax.axis_index("section") == 0
    dec_rows_at = lax.axis_index("mp") * dec_rows + jnp.arange(dec_rows, dtype=jnp.int32)
    half_enc = enc_width // 2
    half_dec = dec_width // 2

    def micro_step(step_index, carry_all):
        enc_acc, dec_acc, out_store, grad_store = carry_all
        stream_in = jnp.where(
            section_first,
            lax.dynamic_index_in_dim(x_visible, step_index, 0, keepdims=False).astype(jnp.float32),
            0.0,
        )
        grid_level = lax.dynamic_index_in_dim(resolution, step_index, 0, keepdims=False)
        chosen = lax.dynamic_index_in_dim(visible_index, step_index, 0, keepdims=False)
        target = lax.dynamic_index_in_dim(cotangent, step_index, 0, keepdims=False)
        shown_count = jnp.where(grid_level == 1, VIS, VIS_SMALL)
        grid_width = jnp.where(grid_level == 1, COLS_BIG, COLS_SMALL)
        filled = jnp.where(grid_level == 1, PATCHES, SMALL_PATCHES)
        seen_valid = jnp.arange(vis_total) < shown_count
        grid_valid = jnp.arange(grid_total) < filled
        top_rows_enc, enc_state = block_forward(
            stream_in, enc_mats, enc_gains, enc_shifts, seen_valid, HD_ENC
        )
        top_low = top_rows_enc.astype(jnp.bfloat16)
        sent_rows = jnp.dot(top_low, projection, preferred_element_type=jnp.float32).astype(
            jnp.bfloat16
        )
        arrived = shifted(sent_rows, "section", 1)
        hit_table = (dec_rows_at[:, None] == chosen[None, :]) & seen_valid[None, :]
        seen_count = jnp.sum(hit_table.astype(jnp.float32), axis=1, keepdims=True)
        live_rows = (dec_rows_at < filled).astype(jnp.float32)[:, None]
        shard_rows = lax.all_gather(arrived, "mp", axis=0, tiled=True)
        shard_count = shard_rows.shape[0]
        columns = chosen
        usable = jnp.arange(shard_count) < shown_count
        place_table = ((dec_rows_at[:, None] == columns[None, :]) & usable[None, :]).astype(
            jnp.bfloat16
        )
        placed = jnp.dot(place_table, shard_rows, preferred_element_type=jnp.float32)
        start_rows = (
            placed
            + (live_rows - seen_count) * mask_token
            + live_rows * sincos_table(dec_rows_at, grid_width, dec_width)
        )
        top_rows_dec, dec_state = block_forward(
            start_rows, dec_mats, dec_gains, dec_shifts, grid_valid, HD_DEC
        )
        grad_start, dec_terms = block_backward(
            target.astype(jnp.float32) * live_rows,
            dec_state,
            dec_mats,
            dec_gains,
            grid_valid,
            HD_DEC,
        )
        grad_low = grad_start.astype(jnp.bfloat16)
        mask_term = jnp.sum((live_rows - seen_count) * grad_low.astype(jnp.float32), axis=0)
        columns = chosen
        usable = jnp.arange(enc_rows * lax.axis_size("mp")) < shown_count
        place_table = ((dec_rows_at[:, None] == columns[None, :]) & usable[None, :]).astype(
            jnp.bfloat16
        )
        lifted = lax.psum_scatter(
            jnp.dot(place_table.T, grad_low, preferred_element_type=jnp.float32).astype(
                jnp.bfloat16
            ),
            "mp",
            scatter_dimension=0,
            tiled=True,
        )
        produced = (top_rows_dec * live_rows).astype(jnp.bfloat16)
        dec_new = (
            dec_terms[0],
            dec_terms[1],
            dec_terms[2],
            dec_terms[3],
            dec_terms[4],
            dec_terms[5],
            mask_term,
        )
        dec_acc = tuple(
            (
                jnp.where(section_first, old_sum, old_sum + new_term)
                for old_sum, new_term in zip(dec_acc, dec_new)
            )
        )
        returned, lower_out = shifted((lifted, produced[:, :half_dec]), "section", -1)
        grad_top = jnp.dot(returned, projection.T, preferred_element_type=jnp.float32)
        projection_term = jnp.dot(top_low.T, returned, preferred_element_type=jnp.float32)
        grad_in, enc_terms = block_backward(
            grad_top, enc_state, enc_mats, enc_gains, seen_valid, HD_ENC
        )
        enc_new = (
            enc_terms[0],
            enc_terms[1],
            enc_terms[2],
            enc_terms[3],
            enc_terms[4],
            enc_terms[5],
            projection_term,
        )
        enc_acc = tuple(
            (
                jnp.where(section_first, old_sum + new_term, old_sum)
                for old_sum, new_term in zip(enc_acc, enc_new)
            )
        )
        upper_grad = shifted(grad_in[:, half_enc:].astype(jnp.bfloat16), "section", 1).astype(
            jnp.float32
        )
        out_piece = jnp.where(section_first, lower_out, produced[:, half_dec:])
        grad_piece = jnp.where(section_first, grad_in[:, :half_enc], upper_grad)
        out_store = lax.dynamic_update_index_in_dim(out_store, out_piece, step_index, 0)
        grad_store = lax.dynamic_update_index_in_dim(grad_store, grad_piece, step_index, 0)
        return (enc_acc, dec_acc, out_store, grad_store)

    enc_init = (
        jnp.zeros(enc_mats[0].shape, jnp.float32),
        jnp.zeros(enc_mats[1].shape, jnp.float32),
        jnp.zeros(enc_mats[2].shape, jnp.float32),
        jnp.zeros(enc_mats[3].shape, jnp.float32),
        jnp.zeros((2, enc_width), jnp.float32),
        jnp.zeros((2, enc_width), jnp.float32),
        jnp.zeros(projection.shape, jnp.float32),
    )
    dec_init = (
        jnp.zeros(dec_mats[0].shape, jnp.float32),
        jnp.zeros(dec_mats[1].shape, jnp.float32),
        jnp.zeros(dec_mats[2].shape, jnp.float32),
        jnp.zeros(dec_mats[3].shape, jnp.float32),
        jnp.zeros((2, dec_width), jnp.float32),
        jnp.zeros((2, dec_width), jnp.float32),
        jnp.zeros((dec_width,), jnp.float32),
    )
    out_init = jnp.zeros((micro_count, dec_rows, half_dec), jnp.bfloat16)
    grad_init = jnp.zeros((micro_count, enc_rows, half_enc), jnp.float32)
    enc_acc, dec_acc, out_store, grad_store = lax.fori_loop(
        0, micro_count, micro_step, (enc_init, dec_init, out_init, grad_init)
    )
    grad_mats = (
        enc_acc[0],
        enc_acc[1],
        enc_acc[2],
        enc_acc[3],
        dec_acc[0],
        dec_acc[1],
        dec_acc[2],
        dec_acc[3],
    )
    summed = (
        lax.psum_scatter(grad_mats[0], ("section", "dp"), scatter_dimension=0, tiled=True),
        lax.psum_scatter(grad_mats[1], ("section", "dp"), scatter_dimension=1, tiled=True),
        lax.psum_scatter(grad_mats[2], ("section", "dp"), scatter_dimension=0, tiled=True),
        lax.psum_scatter(grad_mats[3], ("section", "dp"), scatter_dimension=1, tiled=True),
        lax.psum_scatter(grad_mats[4], ("section", "dp"), scatter_dimension=0, tiled=True),
        lax.psum_scatter(grad_mats[5], ("section", "dp"), scatter_dimension=1, tiled=True),
        lax.psum_scatter(grad_mats[6], ("section", "dp"), scatter_dimension=0, tiled=True),
        lax.psum_scatter(grad_mats[7], ("section", "dp"), scatter_dimension=1, tiled=True),
    )
    small_sums = lax.psum(
        (enc_acc[4], enc_acc[5], enc_acc[6], dec_acc[6], dec_acc[4], dec_acc[5]),
        ("section", "dp", "mp"),
    )
    return (
        out_store,
        grad_store,
        summed[0],
        summed[1],
        summed[2],
        summed[3],
        small_sums[0],
        small_sums[1],
        small_sums[2],
        small_sums[3],
        summed[4],
        summed[5],
        summed[6],
        summed[7],
        small_sums[4],
        small_sums[5],
    )


def solution(mesh):
    return jax.shard_map(
        per_device,
        mesh=mesh,
        in_specs=(
            P("dp", "mp", None),
            P("dp"),
            P("dp", None),
            P(("section", "dp"), None, "mp"),
            P("mp", ("section", "dp")),
            P(("section", "dp"), "mp"),
            P("mp", ("section", "dp")),
            P(),
            P(),
            P(),
            P(),
            P(("section", "dp"), None, "mp"),
            P("mp", ("section", "dp")),
            P(("section", "dp"), "mp"),
            P("mp", ("section", "dp")),
            P(),
            P(),
            P("dp", "mp", None),
        ),
        out_specs=(
            P("dp", "mp", "section"),
            P("dp", "mp", "section"),
            P(("section", "dp"), None, "mp"),
            P("mp", ("section", "dp")),
            P(("section", "dp"), "mp"),
            P("mp", ("section", "dp")),
            P(),
            P(),
            P(),
            P(),
            P(("section", "dp"), None, "mp"),
            P("mp", ("section", "dp")),
            P(("section", "dp"), "mp"),
            P("mp", ("section", "dp")),
            P(),
            P(),
        ),
        check_vma=False,
    )
```

profile of v0, /device:TPU:0, one launch (start us, length us, event | category | flops | bytes accessed | tf_op | source)
XLA Modules:
  0.0 2780.2 jit_solution(1376104867276816824)
XLA Ops:
  9.7 32.8 %all_gather.119 = bf16[128,512]{0,1:T(8,128)(2,1)S(1)} all-gather(bf16[128,64]{0,1:T(8,128)(2,1)} %param.36), channel_id=1, replica_groups=mesh['section'=2,'dp'=4,'mp'=4] {'section','dp'}, dimensions={1}, use_global_device_ids=true | all-gather | bytes 147456 | tf_op jit(solution)/shard_map/all_gather | solution.py:254
  44.4 32.4 %all_gather.115 = bf16[192,768]{0,1:T(8,128)(2,1)S(1)} all-gather(bf16[192,96]{0,1:T(8,128)(2,1)S(1)} %copy.128), channel_id=1, replica_groups=mesh['section'=2,'dp'=4,'mp'=4] {'section','dp'}, dimensions={1}, use_global_device_ids=true | all-gather | bytes 331776 | tf_op jit(solution)/shard_map/all_gather | solution.py:250
  76.9 33.5 %all_gather.118 = bf16[512,3,128]{2,0,1:T(8,128)(2,1)S(1)} all-gather(bf16[64,3,128]{2,0,1:T(8,128)(2,1)} %param.35), channel_id=1, replica_groups=mesh['section'=2,'dp'=4,'mp'=4] {'section','dp'}, dimensions={0}, use_global_device_ids=true | all-gather | bytes 442368 | tf_op jit(solution)/shard_map/all_gather | solution.py:253
  110.6 32.9 %all_gather.121 = bf16[512,512]{0,1:T(8,128)(2,1)S(1)} all-gather(bf16[512,64]{0,1:T(8,128)(2,1)S(1)} %copy-done.138), channel_id=1, replica_groups=mesh['section'=2,'dp'=4,'mp'=4] {'section','dp'}, dimensions={1}, use_global_device_ids=true | all-gather | bytes 589824 | tf_op jit(solution)/shard_map/all_gather | solution.py:256
  144.6 39.0 %all_gather.114 = bf16[768,3,192]{2,1,0:T(4,128)(2,1)} all-gather(bf16[96,3,192]{2,1,0:T(4,128)(2,1)S(1)} %copy.127), channel_id=1, replica_groups=mesh['section'=2,'dp'=4,'mp'=4] {'section','dp'}, dimensions={0}, use_global_device_ids=true | all-gather | bytes 995328 | tf_op jit(solution)/shard_map/all_gather | solution.py:249
  186.4 33.9 %all_gather.120 = bf16[512,512]{1,0:T(8,128)(2,1)} all-gather(bf16[64,512]{1,0:T(8,128)(2,1)S(1)} %copy-done.139), channel_id=1, replica_groups=mesh['section'=2,'dp'=4,'mp'=4] {'section','dp'}, dimensions={0}, use_global_device_ids=true | all-gather | bytes 589824 | tf_op jit(solution)/shard_map/all_gather | solution.py:255
  222.6 1862.7 %while.172 = (s32[]{:T(128)}, f32[768,3,192]{0,2,1:T(8,128)}, f32[192,768]{1,0:T(8,128)}, f32[768,768]{1,0:T(8,128)}, f32[768,768]{1,0:T(8,128)}, /*index=5*/f32...) while((s32[]{:T(128)}, f32[768,3,192]{0,2,1:T(8,128)}, ...), condition=%wide.region_46.47_spmd.clone.clone.clone, body=%wide.region_0.46_spmd.clone.clone.clone.sunk | while | flops 18765557760 | bytes 968249408 | solution.py:403
  241.1 29.0 %reduce-scatter.36.cloned.1.call-done = f32[128,768]{1,0:T(8,128)} async-done(((f32[512,768]{1,0:T(8,128)}), f32[128,768]{1,0:T(8,128)}) %reduce-scatter.36.cloned.1.call-update) | async-done | bytes 393232 | tf_op jit(solution)/shard_map/while/body/eval_jaxpr/reduce_scatter | solution.py:62
  335.9 23.9 all-gather.11.cloned.1.call-done
  362.8 56.1 %while.173 = (s32[]{:T(128)}, bf16[4,512,128]{2,1,0:T(8,128)(2,1)S(1)}, f32[4,4,512]{2,1,0:T(4,128)S(1)}, s32[4]{0:T(128)S(1)}, bf16[2048,4,32]{0,2,1:T(8,128)(2...) while((s32[]{:T(128)}, ...), condition=%wide.region_15.15_spmd.clone, body=%wide.region_12.14_spmd.clone.sunk | while | flops 587268096 | bytes 52240560 | solution.py:102
  422.6 44.6 %reduce-scatter.40.cloned.1.call-done = f32[512,512]{0,1:T(8,128)} async-done(((f32[2048,512]{0,1:T(8,128)}), f32[512,512]{0,1:T(8,128)}) %reduce-scatter.40.cloned.1.call-update) | async-done | bytes 1048592 | tf_op jit(solution)/shard_map/while/body/eval_jaxpr/reduce_scatter | solution.py:62
  532.4 39.6 %reduce-scatter.44.cloned.1.call-done = f32[512,512]{0,1:T(8,128)} async-done(((f32[2048,512]{0,1:T(8,128)}), f32[512,512]{0,1:T(8,128)}) %reduce-scatter.44.cloned.1.call-update) | async-done | bytes 1048592 | tf_op jit(solution)/shard_map/while/body/eval_jaxpr/reduce_scatter | solution.py:62
  574.3 44.6 %reduce-scatter.42.cloned.1.call-done = f32[512,512]{0,1:T(8,128)} async-done(((f32[2048,512]{0,1:T(8,128)}), f32[512,512]{0,1:T(8,128)}) %reduce-scatter.42.cloned.1.call-update) | async-done | bytes 1048592 | tf_op jit(solution)/shard_map/while/body/eval_jaxpr/reduce_scatter | solution.py:62
  646.8 303.5 %while.174 = (s32[]{:T(128)}, f32[2048,4,32]{0,2,1:T(8,128)}, f32[2048,4,32]{0,2,1:T(8,128)S(1)}, bf16[4,512,4,32]{1,3,2,0:T(8,128)(2,1)}, s32[4]{0:T(128)S(1)},...) while((s32[]{:T(128)}, f32[2048,4,32]{0,2,1:T(8,128)}, ...), condition=%wide.region_24.24_spmd.clone, body=%wide.region_22.23_spmd.clone.sunk | while | flops 1452353536 | bytes 258150656 | solution.py:156
  666.4 30.9 %fusion.505 = bf16[4,512,4,32]{1,3,2,0:T(8,128)(2,1)} fusion(bf16[4,512,4,32]{1,3,2,0:T(8,128)(2,1)} %get-tuple-element.2404, s32[]{:T(128)S(6)} %copy.187, bf16[2048,4,32]{0,2,1:T(8,128)(2,1)S(1)} %get-tuple-element.2421, f32[4,512,2048]{2,1,0:T(8,128)} %fusion.501, f32[4,512,2048]{2,1,0:T(8,128)} %copy-done, ...), kind=kOutput, calls=%fused_computation.43.clone.1 | convolution fusion | flops 314642432 | bytes 67784704 | tf_op jit(solution)/shard_map/while/body/eval_jaxpr/while/body/eval_jaxpr/hqk,khd->qhd/dot_general | solution.py:138
  697.3 25.3 fusion.503
  741.9 30.9 %fusion.505 = bf16[4,512,4,32]{1,3,2,0:T(8,128)(2,1)} fusion(bf16[4,512,4,32]{1,3,2,0:T(8,128)(2,1)} %get-tuple-element.2404, s32[]{:T(128)S(6)} %copy.187, bf16[2048,4,32]{0,2,1:T(8,128)(2,1)S(1)} %get-tuple-element.2421, f32[4,512,2048]{2,1,0:T(8,128)} %fusion.501, f32[4,512,2048]{2,1,0:T(8,128)} %copy-done, ...), kind=kOutput, calls=%fused_computation.43.clone.1 | convolution fusion | flops 314642432 | bytes 67784704 | tf_op jit(solution)/shard_map/while/body/eval_jaxpr/while/body/eval_jaxpr/hqk,khd->qhd/dot_general | solution.py:138
  772.8 25.5 fusion.503
  817.7 30.9 %fusion.505 = bf16[4,512,4,32]{1,3,2,0:T(8,128)(2,1)} fusion(bf16[4,512,4,32]{1,3,2,0:T(8,128)(2,1)} %get-tuple-element.2404, s32[]{:T(128)S(6)} %copy.187, bf16[2048,4,32]{0,2,1:T(8,128)(2,1)S(1)} %get-tuple-element.2421, f32[4,512,2048]{2,1,0:T(8,128)} %fusion.501, f32[4,512,2048]{2,1,0:T(8,128)} %copy-done, ...), kind=kOutput, calls=%fused_computation.43.clone.1 | convolution fusion | flops 314642432 | bytes 67784704 | tf_op jit(solution)/shard_map/while/body/eval_jaxpr/while/body/eval_jaxpr/hqk,khd->qhd/dot_general | solution.py:138
  848.6 25.5 fusion.503
  893.5 30.9 %fusion.505 = bf16[4,512,4,32]{1,3,2,0:T(8,128)(2,1)} fusion(bf16[4,512,4,32]{1,3,2,0:T(8,128)(2,1)} %get-tuple-element.2404, s32[]{:T(128)S(6)} %copy.187, bf16[2048,4,32]{0,2,1:T(8,128)(2,1)S(1)} %get-tuple-element.2421, f32[4,512,2048]{2,1,0:T(8,128)} %fusion.501, f32[4,512,2048]{2,1,0:T(8,128)} %copy-done, ...), kind=kOutput, calls=%fused_computation.43.clone.1 | convolution fusion | flops 314642432 | bytes 67784704 | tf_op jit(solution)/shard_map/while/body/eval_jaxpr/while/body/eval_jaxpr/hqk,khd->qhd/dot_general | solution.py:138
  924.3 25.5 fusion.503
  958.6 44.6 %reduce-scatter.46.cloned.1.call-done = f32[512,512]{0,1:T(8,128)} async-done(((f32[2048,512]{0,1:T(8,128)}), f32[512,512]{0,1:T(8,128)}) %reduce-scatter.46.cloned.1.call-update) | async-done | bytes 1048592 | tf_op jit(solution)/shard_map/while/body/eval_jaxpr/reduce_scatter | solution.py:62
  1170.0 30.1 %reduce-scatter.36.cloned.1.call-done = f32[128,768]{1,0:T(8,128)} async-done(((f32[512,768]{1,0:T(8,128)}), f32[128,768]{1,0:T(8,128)}) %reduce-scatter.36.cloned.1.call-update) | async-done | bytes 393232 | tf_op jit(solution)/shard_map/while/body/eval_jaxpr/reduce_scatter | solution.py:62
  1266.0 23.9 all-gather.11.cloned.1.call-done
  1292.9 56.1 %while.173 = (s32[]{:T(128)}, bf16[4,512,128]{2,1,0:T(8,128)(2,1)S(1)}, f32[4,4,512]{2,1,0:T(4,128)S(1)}, s32[4]{0:T(128)S(1)}, bf16[2048,4,32]{0,2,1:T(8,128)(2...) while((s32[]{:T(128)}, ...), condition=%wide.region_15.15_spmd.clone, body=%wide.region_12.14_spmd.clone.sunk | while | flops 587268096 | bytes 52240560 | solution.py:102
  1352.7 44.6 %reduce-scatter.40.cloned.1.call-done = f32[512,512]{0,1:T(8,128)} async-done(((f32[2048,512]{0,1:T(8,128)}), f32[512,512]{0,1:T(8,128)}) %reduce-scatter.40.cloned.1.call-update) | async-done | bytes 1048592 | tf_op jit(solution)/shard_map/while/body/eval_jaxpr/reduce_scatter | solution.py:62
  1462.5 39.6 %reduce-scatter.44.cloned.1.call-done = f32[512,512]{0,1:T(8,128)} async-done(((f32[2048,512]{0,1:T(8,128)}), f32[512,512]{0,1:T(8,128)}) %reduce-scatter.44.cloned.1.call-update) | async-done | bytes 1048592 | tf_op jit(solution)/shard_map/while/body/eval_jaxpr/reduce_scatter | solution.py:62
  1504.4 44.8 %reduce-scatter.42.cloned.1.call-done = f32[512,512]{0,1:T(8,128)} async-done(((f32[2048,512]{0,1:T(8,128)}), f32[512,512]{0,1:T(8,128)}) %reduce-scatter.42.cloned.1.call-update) | async-done | bytes 1048592 | tf_op jit(solution)/shard_map/while/body/eval_jaxpr/reduce_scatter | solution.py:62
  1577.0 303.5 %while.174 = (s32[]{:T(128)}, f32[2048,4,32]{0,2,1:T(8,128)}, f32[2048,4,32]{0,2,1:T(8,128)S(1)}, bf16[4,512,4,32]{1,3,2,0:T(8,128)(2,1)}, s32[4]{0:T(128)S(1)},...) while((s32[]{:T(128)}, f32[2048,4,32]{0,2,1:T(8,128)}, ...), condition=%wide.region_24.24_spmd.clone, body=%wide.region_22.23_spmd.clone.sunk | while | flops 1452353536 | bytes 258150656 | solution.py:156
  1596.6 30.9 %fusion.505 = bf16[4,512,4,32]{1,3,2,0:T(8,128)(2,1)} fusion(bf16[4,512,4,32]{1,3,2,0:T(8,128)(2,1)} %get-tuple-element.2404, s32[]{:T(128)S(6)} %copy.187, bf16[2048,4,32]{0,2,1:T(8,128)(2,1)S(1)} %get-tuple-element.2421, f32[4,512,2048]{2,1,0:T(8,128)} %fusion.501, f32[4,512,2048]{2,1,0:T(8,128)} %copy-done, ...), kind=kOutput, calls=%fused_computation.43.clone.1 | convolution fusion | flops 314642432 | bytes 67784704 | tf_op jit(solution)/shard_map/while/body/eval_jaxpr/while/body/eval_jaxpr/hqk,khd->qhd/dot_general | solution.py:138
  1627.5 25.3 fusion.503
  1672.2 30.9 %fusion.505 = bf16[4,512,4,32]{1,3,2,0:T(8,128)(2,1)} fusion(bf16[4,512,4,32]{1,3,2,0:T(8,128)(2,1)} %get-tuple-element.2404, s32[]{:T(128)S(6)} %copy.187, bf16[2048,4,32]{0,2,1:T(8,128)(2,1)S(1)} %get-tuple-element.2421, f32[4,512,2048]{2,1,0:T(8,128)} %fusion.501, f32[4,512,2048]{2,1,0:T(8,128)} %copy-done, ...), kind=kOutput, calls=%fused_computation.43.clone.1 | convolution fusion | flops 314642432 | bytes 67784704 | tf_op jit(solution)/shard_map/while/body/eval_jaxpr/while/body/eval_jaxpr/hqk,khd->qhd/dot_general | solution.py:138
  1703.0 25.5 fusion.503
  1747.9 30.9 %fusion.505 = bf16[4,512,4,32]{1,3,2,0:T(8,128)(2,1)} fusion(bf16[4,512,4,32]{1,3,2,0:T(8,128)(2,1)} %get-tuple-element.2404, s32[]{:T(128)S(6)} %copy.187, bf16[2048,4,32]{0,2,1:T(8,128)(2,1)S(1)} %get-tuple-element.2421, f32[4,512,2048]{2,1,0:T(8,128)} %fusion.501, f32[4,512,2048]{2,1,0:T(8,128)} %copy-done, ...), kind=kOutput, calls=%fused_computation.43.clone.1 | convolution fusion | flops 314642432 | bytes 67784704 | tf_op jit(solution)/shard_map/while/body/eval_jaxpr/while/body/eval_jaxpr/hqk,khd->qhd/dot_general | solution.py:138
  1778.8 25.5 fusion.503
  1823.7 30.9 %fusion.505 = bf16[4,512,4,32]{1,3,2,0:T(8,128)(2,1)} fusion(bf16[4,512,4,32]{1,3,2,0:T(8,128)(2,1)} %get-tuple-element.2404, s32[]{:T(128)S(6)} %copy.187, bf16[2048,4,32]{0,2,1:T(8,128)(2,1)S(1)} %get-tuple-element.2421, f32[4,512,2048]{2,1,0:T(8,128)} %fusion.501, f32[4,512,2048]{2,1,0:T(8,128)} %copy-done, ...), kind=kOutput, calls=%fused_computation.43.clone.1 | convolution fusion | flops 314642432 | bytes 67784704 | tf_op jit(solution)/shard_map/while/body/eval_jaxpr/while/body/eval_jaxpr/hqk,khd->qhd/dot_general | solution.py:138
  1854.5 25.5 fusion.503
  1888.8 44.6 %reduce-scatter.46.cloned.1.call-done = f32[512,512]{0,1:T(8,128)} async-done(((f32[2048,512]{0,1:T(8,128)}), f32[512,512]{0,1:T(8,128)}) %reduce-scatter.46.cloned.1.call-update) | async-done | bytes 1048592 | tf_op jit(solution)/shard_map/while/body/eval_jaxpr/reduce_scatter | solution.py:62
  2099.9 41.0 %all-reduce = (f32[2,768]{1,0:T(2,128)}, f32[2,768]{1,0:T(2,128)}, f32[512]{0:T(512)}, f32[2,512]{1,0:T(2,128)}, f32[2,512]{1,0:T(2,128)}) all-reduce(f32[2,768]{1,0:T(2,128)S(1)} %copy-done.108, f32[2,768]{1,0:T(2,128)S(1)} %copy-done.105, f32[512]{0:T(512)S(1)} %copy-done.137, ...), channel_id=1, replica_groups=mesh['section'=2,'dp'=4,'mp'=4] {'section','dp','mp'}, use_global_device_ids=true, to_apply=%region_51.52 | all-reduce | flops 5632 | bytes 45056 | tf_op jit(solution)/shard_map/psum | solution.py:426
  2154.6 62.7 %reduce-scatter.28.cloned.1.call-done = f32[128,64]{0,1:T(8,128)} async-done(((f32[128,512]{0,1:T(8,128)}), f32[128,64]{0,1:T(8,128)}) %reduce-scatter.28.cloned.1.call-update) | async-done | bytes 32784 | tf_op jit(solution)/shard_map/reduce_scatter | solution.py:422
  2217.3 137.7 %all-reduce.3.cloned.1.call-done = f32[768,512]{1,0:T(8,128)} async-done(((f32[768,512]{1,0:T(8,128)}), f32[768,512]{1,0:T(8,128)}) %all-reduce.3.cloned.1.call-update) | async-done | bytes 1572880 | tf_op jit(solution)/shard_map/psum | solution.py:426
  2355.0 66.4 %reduce-scatter.26.cloned.1.call-done = f32[64,3,128]{2,0,1:T(8,128)} async-done(((f32[512,3,128]{2,0,1:T(8,128)}), f32[64,3,128]{2,0,1:T(8,128)}) %reduce-scatter.26.cloned.1.call-update) | async-done | bytes 98320 | tf_op jit(solution)/shard_map/reduce_scatter | solution.py:421
  2421.4 66.3 %reduce-scatter.30.cloned.1.call-done = f32[64,512]{1,0:T(8,128)} async-done(((f32[512,512]{1,0:T(8,128)}), f32[64,512]{1,0:T(8,128)}) %reduce-scatter.30.cloned.1.call-update) | async-done | bytes 131088 | tf_op jit(solution)/shard_map/reduce_scatter | solution.py:423
  2487.7 66.8 %reduce-scatter.32.cloned.1.call-done = f32[512,64]{0,1:T(8,128)} async-done(((f32[512,512]{0,1:T(8,128)}), f32[512,64]{0,1:T(8,128)}) %reduce-scatter.32.cloned.1.call-update) | async-done | bytes 131088 | tf_op jit(solution)/shard_map/reduce_scatter | solution.py:424
  2554.5 72.1 %reduce-scatter.20.cloned.1.call-done = f32[96,3,192]{2,0,1:T(8,128)} async-done(((f32[768,3,192]{2,0,1:T(8,128)}), f32[96,3,192]{2,0,1:T(8,128)}) %reduce-scatter.20.cloned.1.call-update) | async-done | bytes 221200 | tf_op jit(solution)/shard_map/reduce_scatter | solution.py:417
  2626.6 71.9 %reduce-scatter.22.cloned.1.call-done = f32[96,768]{1,0:T(8,128)} async-done(((f32[768,768]{1,0:T(8,128)}), f32[96,768]{1,0:T(8,128)}) %reduce-scatter.22.cloned.1.call-update) | async-done | bytes 294928 | tf_op jit(solution)/shard_map/reduce_scatter | solution.py:419
  2698.5 72.0 %reduce-scatter.24.cloned.1.call-done = f32[768,96]{0,1:T(8,128)} async-done(((f32[768,768]{0,1:T(8,128)}), f32[768,96]{0,1:T(8,128)}) %reduce-scatter.24.cloned.1.call-update) | async-done | bytes 294928 | tf_op jit(solution)/shard_map/reduce_scatter | solution.py:420
  (1088 shorter events, 956.4 us)
Async XLA Ops:
  7.2 213.1 %all-gather.9.cloned.1.call-start = ((), (), s32[]{:S(2)}) async-start(), calls=%async_computation.18 | async-start | bytes 1327104 | tf_op jit(solution)/shard_map/all_gather | solution.py:252
  7.9 214.7 %all-gather.7.cloned.1.call-start = ((), (), s32[]{:S(2)}) async-start(), calls=%async_computation.17 | async-start | bytes 1327104 | tf_op jit(solution)/shard_map/all_gather | solution.py:251
  223.1 47.0 %reduce-scatter.36.cloned.1.call-start = ((), (), s32[]{:S(2)}) async-start(), calls=%async_computation.28 | async-start | bytes 1966080 | tf_op jit(solution)/shard_map/while/body/eval_jaxpr/reduce_scatter | solution.py:62
  241.0 77.0 %reduce-scatter.38.cloned.1.call-start = ((), (), s32[]{:S(2)}) async-start(), calls=%async_computation.29 | async-start | bytes 1966080 | tf_op jit(solution)/shard_map/while/body/eval_jaxpr/reduce_scatter | solution.py:62
  289.3 70.5 %all-gather.11.cloned.1.call-start = ((), (), s32[]{:S(2)}) async-start(), calls=%async_computation.30 | async-start | bytes 2621440 | tf_op jit(solution)/shard_map/while/body/eval_jaxpr/all_gather | solution.py:58
  319.4 6.1 collective-permute-start
  335.5 131.8 %reduce-scatter.40.cloned.1.call-start = ((), (), s32[]{:S(2)}) async-start(), calls=%async_computation.31 | async-start | bytes 5242880 | tf_op jit(solution)/shard_map/while/body/eval_jaxpr/reduce_scatter | solution.py:62
  422.5 70.1 %all-gather.13.cloned.1.call-start = ((), (), s32[]{:S(2)}) async-start(), calls=%async_computation.32 | async-start | bytes 2621440 | tf_op jit(solution)/shard_map/while/body/eval_jaxpr/all_gather | solution.py:58
  468.6 150.3 %copy-start.1 = (f32[512,512]{0,1:T(8,128)}, f32[512,512]{0,1:T(8,128)S(1)}, u32[]{:S(2)}) copy-start(f32[512,512]{0,1:T(8,128)S(1)} %get-tuple-element.2290) | copy-start | bytes 3145732 | tf_op jit(solution)/shard_map/while
  469.9 47.0 %all-gather.15.cloned.1.call-start = ((), (), s32[]{:S(2)}) async-start(), calls=%async_computation.34 | async-start | bytes 2621440 | tf_op jit(solution)/shard_map/while/body/eval_jaxpr/all_gather | solution.py:58
  472.3 99.8 %reduce-scatter.44.cloned.1.call-start = ((), (), s32[]{:S(2)}) async-start(), calls=%async_computation.35 | async-start | bytes 5242880 | tf_op jit(solution)/shard_map/while/body/eval_jaxpr/reduce_scatter | solution.py:62
  527.4 91.6 %reduce-scatter.42.cloned.1.call-start = ((), (), s32[]{:S(2)}) async-start(), calls=%async_computation.33 | async-start | bytes 5242880 | tf_op jit(solution)/shard_map/while/body/eval_jaxpr/reduce_scatter | solution.py:62
  532.4 112.4 %all-gather.17.cloned.1.call-start = ((), (), s32[]{:S(2)}) async-start(), calls=%async_computation.36 | async-start | bytes 2621440 | tf_op jit(solution)/shard_map/while/body/eval_jaxpr/all_gather | solution.py:58
  622.0 381.2 %reduce-scatter.46.cloned.1.call-start = ((), (), s32[]{:S(2)}) async-start(), calls=%async_computation.37 | async-start | bytes 5242880 | tf_op jit(solution)/shard_map/while/body/eval_jaxpr/reduce_scatter | solution.py:62
  958.6 73.1 %reduce-scatter.48.cloned.1.call-start = ((), (), s32[]{:S(2)}) async-start(), calls=%async_computation.38 | async-start | bytes 655360 | tf_op jit(solution)/shard_map/while/body/eval_jaxpr/reduce_scatter | solution.py:329
  1009.9 73.0 %reduce-scatter.50.cloned.1.call-start = ((), (), s32[]{:S(2)}) async-start(), calls=%async_computation.39 | async-start | bytes 1966080 | tf_op jit(solution)/shard_map/while/body/eval_jaxpr/reduce_scatter | solution.py:62
  1031.7 7.3 collective-permute-start.1
  1054.5 88.9 %reduce-scatter.52.cloned.1.call-start = ((), (), s32[]{:S(2)}) async-start(), calls=%async_computation.40 | async-start | bytes 1966080 | tf_op jit(solution)/shard_map/while/body/eval_jaxpr/reduce_scatter | solution.py:62
  1058.5 10.5 collective-permute-start.2
  1145.9 5.6 collective-permute-start.3
  1152.4 47.7 %reduce-scatter.36.cloned.1.call-start = ((), (), s32[]{:S(2)}) async-start(), calls=%async_computation.28 | async-start | bytes 1966080 | tf_op jit(solution)/shard_map/while/body/eval_jaxpr/reduce_scatter | solution.py:62
  1170.0 78.1 %reduce-scatter.38.cloned.1.call-start = ((), (), s32[]{:S(2)}) async-start(), calls=%async_computation.29 | async-start | bytes 1966080 | tf_op jit(solution)/shard_map/while/body/eval_jaxpr/reduce_scatter | solution.py:62
  1219.4 70.5 %all-gather.11.cloned.1.call-start = ((), (), s32[]{:S(2)}) async-start(), calls=%async_computation.30 | async-start | bytes 2621440 | tf_op jit(solution)/shard_map/while/body/eval_jaxpr/all_gather | solution.py:58
  1249.4 6.1 collective-permute-start
  1265.5 131.7 %reduce-scatter.40.cloned.1.call-start = ((), (), s32[]{:S(2)}) async-start(), calls=%async_computation.31 | async-start | bytes 5242880 | tf_op jit(solution)/shard_map/while/body/eval_jaxpr/reduce_scatter | solution.py:62
  1352.6 70.1 %all-gather.13.cloned.1.call-start = ((), (), s32[]{:S(2)}) async-start(), calls=%async_computation.32 | async-start | bytes 2621440 | tf_op jit(solution)/shard_map/while/body/eval_jaxpr/all_gather | solution.py:58
  1398.7 150.5 %copy-start.1 = (f32[512,512]{0,1:T(8,128)}, f32[512,512]{0,1:T(8,128)S(1)}, u32[]{:S(2)}) copy-start(f32[512,512]{0,1:T(8,128)S(1)} %get-tuple-element.2290) | copy-start | bytes 3145732 | tf_op jit(solution)/shard_map/while
  1398.7 150.5 %copy-start.68 = (f32[512]{0:T(512)}, f32[512]{0:T(512)S(1)}, u32[]{:S(2)}) copy-start(f32[512]{0:T(512)S(1)} %broadcast_multiply_fusion.26) | copy-start | bytes 6148 | tf_op jit(solution)/shard_map/while
  1400.0 47.0 %all-gather.15.cloned.1.call-start = ((), (), s32[]{:S(2)}) async-start(), calls=%async_computation.34 | async-start | bytes 2621440 | tf_op jit(solution)/shard_map/while/body/eval_jaxpr/all_gather | solution.py:58
  1402.3 99.8 %reduce-scatter.44.cloned.1.call-start = ((), (), s32[]{:S(2)}) async-start(), calls=%async_computation.35 | async-start | bytes 5242880 | tf_op jit(solution)/shard_map/while/body/eval_jaxpr/reduce_scatter | solution.py:62
  1457.5 91.7 %reduce-scatter.42.cloned.1.call-start = ((), (), s32[]{:S(2)}) async-start(), calls=%async_computation.33 | async-start | bytes 5242880 | tf_op jit(solution)/shard_map/while/body/eval_jaxpr/reduce_scatter | solution.py:62
  1462.4 112.6 %all-gather.17.cloned.1.call-start = ((), (), s32[]{:S(2)}) async-start(), calls=%async_computation.36 | async-start | bytes 2621440 | tf_op jit(solution)/shard_map/while/body/eval_jaxpr/all_gather | solution.py:58
  1552.2 381.2 %reduce-scatter.46.cloned.1.call-start = ((), (), s32[]{:S(2)}) async-start(), calls=%async_computation.37 | async-start | bytes 5242880 | tf_op jit(solution)/shard_map/while/body/eval_jaxpr/reduce_scatter | solution.py:62
  1888.8 73.2 %reduce-scatter.48.cloned.1.call-start = ((), (), s32[]{:S(2)}) async-start(), calls=%async_computation.38 | async-start | bytes 655360 | tf_op jit(solution)/shard_map/while/body/eval_jaxpr/reduce_scatter | solution.py:329
  1940.1 73.0 %reduce-scatter.50.cloned.1.call-start = ((), (), s32[]{:S(2)}) async-start(), calls=%async_computation.39 | async-start | bytes 1966080 | tf_op jit(solution)/shard_map/while/body/eval_jaxpr/reduce_scatter | solution.py:62
  1961.9 7.3 collective-permute-start.1
  1984.7 88.9 %reduce-scatter.52.cloned.1.call-start = ((), (), s32[]{:S(2)}) async-start(), calls=%async_computation.40 | async-start | bytes 1966080 | tf_op jit(solution)/shard_map/while/body/eval_jaxpr/reduce_scatter | solution.py:62
  1988.8 10.5 collective-permute-start.2
  2076.1 5.6 collective-permute-start.3
  2085.4 67.6 %reduce-scatter.34.cloned.1.call-start = ((), (), s32[]{:S(2)}) async-start(), calls=%async_computation.27 | async-start | bytes 884736
  2087.8 129.5 %reduce-scatter.28.cloned.1.call-start = ((), (), s32[]{:S(2)}) async-start(), calls=%async_computation.24 | async-start | bytes 294912 | tf_op jit(solution)/shard_map/reduce_scatter | solution.py:422
  2089.7 265.3 %all-reduce.3.cloned.1.call-start = ((), (), s32[]{:S(2)}) async-start(), calls=%async_computation.22 | async-start | bytes 3145728 | tf_op jit(solution)/shard_map/psum | solution.py:426
  2090.4 331.0 %reduce-scatter.26.cloned.1.call-start = ((), (), s32[]{:S(2)}) async-start(), calls=%async_computation.23 | async-start | bytes 884736 | tf_op jit(solution)/shard_map/reduce_scatter | solution.py:421
  2091.2 396.6 %reduce-scatter.30.cloned.1.call-start = ((), (), s32[]{:S(2)}) async-start(), calls=%async_computation.25 | async-start | bytes 1179648 | tf_op jit(solution)/shard_map/reduce_scatter | solution.py:423
  2091.8 462.8 %reduce-scatter.32.cloned.1.call-start = ((), (), s32[]{:S(2)}) async-start(), calls=%async_computation.26 | async-start | bytes 1179648 | tf_op jit(solution)/shard_map/reduce_scatter | solution.py:424
  2093.2 533.4 %reduce-scatter.20.cloned.1.call-start = ((), (), s32[]{:S(2)}) async-start(), calls=%async_computation.19 | async-start | bytes 2654208 | tf_op jit(solution)/shard_map/reduce_scatter | solution.py:417
  2096.2 602.3 %reduce-scatter.22.cloned.1.call-start = ((), (), s32[]{:S(2)}) async-start(), calls=%async_computation.20 | async-start | bytes 2654208 | tf_op jit(solution)/shard_map/reduce_scatter | solution.py:419
  2096.8 673.7 %reduce-scatter.24.cloned.1.call-start = ((), (), s32[]{:S(2)}) async-start(), calls=%async_computation.21 | async-start | bytes 2654208 | tf_op jit(solution)/shard_map/reduce_scatter | solution.py:420
  (284 other events, 5450.7 us)
Sparse Core Ops, SparseCore 0:
  10.1 45.3 all-gather.8
  57.6 41.5 all-gather.6
  241.1 28.9 reduce-scatter.35
  289.5 28.5 reduce-scatter.37
  335.6 24.2 all-gather.10
  422.6 44.5 reduce-scatter.39
  470.0 22.5 all-gather.12
  494.3 22.5 all-gather.14
  527.5 44.4 reduce-scatter.43
  574.4 44.4 reduce-scatter.41
  622.1 22.5 all-gather.16
  958.7 44.5 reduce-scatter.45
  1010.1 21.6 reduce-scatter.47
  1054.6 28.2 reduce-scatter.49
  1114.8 28.5 reduce-scatter.51
  1170.1 30.0 reduce-scatter.35
  1219.5 28.5 reduce-scatter.37
  1265.6 24.2 all-gather.10
  1352.7 44.4 reduce-scatter.39
  1400.1 22.5 all-gather.12
  1424.4 22.5 all-gather.14
  1457.6 44.4 reduce-scatter.43
  1504.6 44.4 reduce-scatter.41
  1552.3 22.5 all-gather.16
  1888.9 44.4 reduce-scatter.45
  1940.2 21.6 reduce-scatter.47
  1984.8 28.2 reduce-scatter.49
  2045.0 28.5 reduce-scatter.51
  2089.5 63.3 reduce-scatter.33
  2157.1 60.1 reduce-scatter.27
  2224.0 130.9 all-reduce.2
  2359.3 62.0 reduce-scatter.25
  2425.2 62.4 reduce-scatter.29
  2492.1 62.3 reduce-scatter.31
  2558.6 67.9 reduce-scatter.19
  2630.5 67.9 reduce-scatter.21
  2702.4 67.9 reduce-scatter.23
where the time goes:
time: 2790 us; the launch traced here: 2780 us
  waiting for transfers between devices  1360 us (49%)
  matrix products  817 us (29%)
  blocking collectives  323 us (12%)
  other arithmetic  99.9 us (4%)
  local copies, waits for them, and re-layouts  98.7 us (4%)
  loops' own time  42.6 us (2%)
    reduce_scatter x16, waiting for transfers between devices, spread(): lax.psum_scatter(jnp.dot(left_rows, weight, preferred_element_type=jnp.fl...  495 us
    dot_general x10, matrix products, one_block(): jnp.einsum('hqk,khd->qhd', grad_raw, key_rows, preferred_element_type=jnp...  256 us
    dot_general x10, matrix products, one_block(): jnp.einsum('hqk,qhd->khd', grad_raw, query_block, preferred_element_type=...  214 us
    all_gather x8, waiting for transfers between devices, collect(): return lax.all_gather(rows_low, 'mp', axis=0, tiled=True)  155 us
    psum x1, waiting for transfers between devices, per_device(): lax.psum((enc_acc[4], enc_acc[5], enc_acc[6], dec_acc[6], dec_acc[4], dec...  138 us
    dot_general x10, matrix products, one_block(): jnp.einsum('qhd,khd->hqk', grad_block, value_rows, preferred_element_type...  72.5 us
    reduce_scatter x1, waiting for transfers between devices, per_device(): lax.psum_scatter(grad_mats[0], ('section', 'dp'), scatter_dimension=0, ti...  72.1 us
    reduce_scatter x1, waiting for transfers between devices, per_device(): lax.psum_scatter(grad_mats[3], ('section', 'dp'), scatter_dimension=1, ti...  72 us
  transfers between devices with their start and end apart: 45, of which 43 were waited for; matrix products, arithmetic and copies ran while one was open for 4% of the time, Pallas kernels for 0%

commit v1 on v0

v1 whole, which is shorter than its diff:
```python
import functools
import math

import jax
import jax.numpy as jnp
import numpy as np
from jax import lax
from jax.experimental import pallas as pl
from jax.experimental.pallas import tpu as pltpu
from jax.sharding import PartitionSpec as P

HD_ENC = 64
HD_DEC = 32
COLS_SMALL = 32
COLS_BIG = 64
PATCHES = 2048
SMALL_PATCHES = 512
VIS = 512
VIS_SMALL = 128

MESH = pl.DeviceIdType.MESH
bf = jnp.bfloat16
f32 = jnp.float32
LOG2E = 1.4426950408889634
NEG = -1e30


def nn(a, b):
    return lax.dot_general(a, b, (((1,), (0,)), ((), ())), preferred_element_type=f32)


def nt(a, b):
    return lax.dot_general(a, b, (((1,), (1,)), ((), ())), preferred_element_type=f32)


def tn(a, b):
    return lax.dot_general(a, b, (((0,), (0,)), ((), ())), preferred_element_type=f32)


def norm_stats(stream):
    centre = stream - jnp.mean(stream, axis=-1, keepdims=True)
    inverse = lax.rsqrt(jnp.mean(centre * centre, axis=-1, keepdims=True) + 1e-06)
    return centre * inverse, inverse


def normalize(stream, gain, shift):
    scaled, _ = norm_stats(stream)
    return scaled * gain + shift


def normalize_back(stream, gain, grad_out):
    scaled, inverse = norm_stats(stream)
    f = grad_out * gain
    grad_in = inverse * (
        f
        - jnp.mean(f, axis=-1, keepdims=True)
        - scaled * jnp.mean(f * scaled, axis=-1, keepdims=True)
    )
    return (
        grad_in,
        jnp.sum(grad_out * scaled, axis=0, keepdims=True),
        jnp.sum(grad_out, axis=0, keepdims=True),
    )


def gelu_and_slope(a):
    x = jnp.abs(a) * 0.7071067811865476
    t = 1.0 / (1.0 + 0.3275911 * x)
    e = jnp.exp2(x * x * (-LOG2E))
    poly = ((((1.061405429 * t - 1.453152027) * t + 1.421413741) * t - 0.284496736) * t + 0.254829592) * t
    tail = 0.5 * poly * e
    phi = jnp.where(a >= 0, 1.0 - tail, tail)
    return a * phi, phi + a * e * 0.3989422804014327


class Ctx:
    def __init__(self, ss, rs, dp):
        self.ss, self.rs, self.n, self.dp = ss, rs, 0, dp
        self.s = lax.axis_index("section")
        self.d = lax.axis_index("dp")
        self.m = lax.axis_index("mp")
        m = self.m
        self.lo = lax.rem(m, 2)
        self.hi = m // 2
        self.m1 = m + 1 - 2 * self.lo
        self.m2 = lax.rem(m + 2, 4)
        self.m3 = lax.rem(self.m1 + 2, 4)
        self.core = {"mp": self.m1}
        self.y = {"mp": self.m2}
        self.x = {"section": 1 - self.s}
        self.pending = []

    def z(self, k):
        return {"dp": lax.rem(self.d + k, self.dp)}

    def barrier(self, peers):
        b = pltpu.get_barrier_semaphore()
        for p in peers:
            pl.semaphore_signal(b, inc=1, device_id=p, device_id_type=MESH)
        pl.semaphore_wait(b, len(peers))

    def send(self, src, dst, dev):
        i = self.n
        self.n += 1
        c = pltpu.make_async_remote_copy(
            src_ref=src,
            dst_ref=dst,
            send_sem=self.ss.at[i],
            recv_sem=self.rs.at[i],
            device_id=dev,
            device_id_type=MESH,
        )
        c.start()
        self.pending.append(c)
        return c

    def drain(self):
        for c in self.pending:
            c.wait_send()
        self.pending = []


class GatherMp:
    def __init__(self, cx, buf):
        self.cx, self.buf = cx, buf
        m = cx.m
        self.c2 = cx.send(buf.at[m], buf.at[m], cx.y)
        self.c1 = cx.send(buf.at[m], buf.at[m], cx.core)

    def forward(self):
        cx, buf = self.cx, self.buf
        self.c2.wait_recv()
        self.c3 = cx.send(buf.at[cx.m2], buf.at[cx.m2], cx.core)

    def near(self):
        self.c1.wait_recv()

    def far(self):
        self.c3.wait_recv()

    def finish(self):
        self.forward()
        self.near()
        self.far()


def reduce_mp(cx, part, stage, recv):
    stage[0] = part[cx.m3].astype(bf)
    c3 = cx.send(stage.at[0], recv.at[0], cx.core)
    stage[1] = part[cx.m1].astype(bf)
    c1 = cx.send(stage.at[1], recv.at[1], cx.core)
    c3.wait_recv()
    stage[2] = (part[cx.m2] + recv[0].astype(f32)).astype(bf)
    c2 = cx.send(stage.at[2], recv.at[2], cx.y)
    c1.wait_recv()
    own = part[cx.m] + recv[1].astype(f32)
    c2.wait_recv()
    return own + recv[2].astype(f32)


class GatherW:
    def __init__(self, cx, shard, whole):
        self.cx, self.whole, self.rows = cx, whole, shard.shape[0]
        own = self.at(cx.s, cx.d)
        self.zs = [cx.send(shard, own, cx.z(k)) for k in range(1, cx.dp)]
        self.xs = [cx.send(shard, own, cx.x)]
        own[...] = shard[...]

    def at(self, s, d):
        start = (s * self.cx.dp + d) * self.rows
        return self.whole.at[pl.ds(pl.multiple_of(start, 16), self.rows)]

    def forward(self):
        cx = self.cx
        for k in range(1, cx.dp):
            self.zs[k - 1].wait_recv()
            block = self.at(cx.s, lax.rem(cx.d + cx.dp - k, cx.dp))
            self.xs.append(cx.send(block, block, cx.x))

    def finish(self):
        for c in self.xs:
            c.wait_recv()


class ScatterW:
    def __init__(self, cx, rows, out, xs, xr, zs, zr):
        self.cx, self.rows, self.out = cx, rows, out
        self.xs, self.xr, self.zs, self.zr = xs, xr, zs, zr

    def section(self, s):
        size = self.cx.dp * self.rows
        return pl.ds(pl.multiple_of(s * size, 16), size)

    def start(self, part):
        cx = self.cx
        self.part = part
        self.xs[...] = part[self.section(1 - cx.s), :].astype(bf)
        self.cx_copy = cx.send(self.xs, self.xr, cx.x)

    def middle(self):
        cx, rows = self.cx, self.rows
        self.cx_copy.wait_recv()
        total = self.part[self.section(cx.s), :] + self.xr[...].astype(f32)
        self.zs[...] = total.astype(bf)
        self.copies = []
        for k in range(1, cx.dp):
            to = lax.rem(cx.d + k, cx.dp)
            block = self.zs.at[pl.ds(pl.multiple_of(to * rows, 16), rows)]
            self.copies.append(cx.send(block, self.zr.at[k - 1], cx.z(k)))

    def finish(self):
        cx, rows = self.cx, self.rows
        start = (cx.s * cx.dp + cx.d) * rows
        mine = pl.ds(pl.multiple_of(cx.d * rows, 16), rows)
        own = self.part[pl.ds(pl.multiple_of(start, 16), rows), :] + self.xr[mine, :].astype(f32)
        for k in range(1, cx.dp):
            self.copies[k - 1].wait_recv()
            own = own + self.zr[k - 1].astype(f32)
        self.out[...] = own


def iota(shape, dim):
    return lax.broadcasted_iota(jnp.int32, shape, dim)


def enc_forward_kernel(dp, gather, *refs):
    it = iter(refs)
    take = lambda n: [next(it) for _ in range(n)]
    res, x_all, gains, shifts, proj = take(5)
    shards = take(6)
    if gather:
        wa, wb, wc, wd, we, wf = take(6)
    else:
        wa, wb, wc = shards[:3]
        wd, we, wf = take(3)
    n1, n2, qkv, ctx, slope, active, mid_out, top_out, low_all = take(9)
    ss, rs, part, stage, recv = take(5)
    cx = Ctx(ss, rs, dp)
    peers = [cx.core, cx.y]
    if gather:
        peers += [cx.x] + [cx.z(k) for k in range(1, dp)]
    cx.barrier(peers)
    if gather:
        ga = GatherW(cx, shards[0], wa)
    stream = x_all[cx.s].astype(f32)
    n1[cx.m] = normalize(stream, gains[0:1, :], shifts[0:1, :]).astype(bf)
    g1 = GatherMp(cx, n1)
    if gather:
        gb = GatherW(cx, shards[1], wb)
        gc = GatherW(cx, shards[2], wc)
    g1.finish()
    if gather:
        ga.forward()
        gd = GatherW(cx, shards[3], wd.at[0])
        ge = GatherW(cx, shards[4], we.at[0])
        gf = GatherW(cx, shards[5], wf.at[0])
        ga.finish()
    rows = n1.shape[1]
    total = 4 * rows
    width = n1.shape[2]
    n1_all = n1[...].reshape(total, width)
    qkv[...] = nn(n1_all, wa[...]).astype(bf)
    if gather:
        gb.forward()
    shown = jnp.where(res[cx.s] == 1, VIS, VIS_SMALL)
    bias = jnp.where(iota((1, total), 1) < shown, 0.0, NEG)
    scale2 = HD_ENC**-0.5 * LOG2E
    heads = (width // 4) // HD_ENC
    pieces = [jnp.zeros((total, HD_ENC), bf)]
    for h in range(heads):
        q = qkv[:, h * HD_ENC : (h + 1) * HD_ENC]
        k = qkv[:, (heads + h) * HD_ENC : (heads + h + 1) * HD_ENC]
        v = qkv[:, (2 * heads + h) * HD_ENC : (2 * heads + h + 1) * HD_ENC]
        sc = nt(q, k) + bias
        top = jnp.max(sc, axis=1, keepdims=True)
        e = jnp.exp2((sc - top) * scale2)
        tot = jnp.sum(e, axis=1, keepdims=True)
        pieces.append((nn(e.astype(bf), v) / tot).astype(bf))
    ctx[...] = jnp.concatenate(pieces, axis=1)
    if gather:
        gc.forward()
    cpad = ctx.shape[1]
    part[...] = nt(ctx[...], wa[:, width - cpad :]).reshape(part.shape)
    mid = stream + reduce_mp(cx, part, stage.at[0], recv.at[0])
    mid_out[...] = mid
    n2[cx.m] = normalize(mid, gains[1:2, :], shifts[1:2, :]).astype(bf)
    g2 = GatherMp(cx, n2)
    if gather:
        gb.finish()
    g2.finish()
    hid = nn(n2[...].reshape(total, width), wb[...])
    act, slo = gelu_and_slope(hid)
    active[...] = act.astype(bf)
    slope[...] = slo.astype(bf)
    if gather:
        gd.forward()
        gc.finish()
    part[...] = nt(active[...], wc[...]).reshape(part.shape)
    top = (mid_out[...] + reduce_mp(cx, part, stage.at[1], recv.at[1])).astype(bf)
    top_out[...] = top
    low_all[cx.m] = nn(top, proj[...]).astype(bf)
    g3 = GatherMp(cx, low_all)
    if gather:
        ge.forward()
        gf.forward()
        gd.finish()
        yd = cx.send(wd.at[0], wd.at[1], cx.y)
    else:
        for w, sh in zip((wd, we, wf), shards[3:]):
            w[0] = sh[...]
        yd = cx.send(wd.at[0], wd.at[1], cx.y)
    g3.finish()
    if gather:
        ge.finish()
    ye = cx.send(we.at[0], we.at[1], cx.y)
    if gather:
        gf.finish()
    yf = cx.send(wf.at[0], wf.at[1], cx.y)
    yd.wait_recv()
    ye.wait_recv()
    yf.wait_recv()
    cx.drain()


def vm(n):
    return [pl.BlockSpec(memory_space=pltpu.VMEM)] * n


SMEM = pl.BlockSpec(memory_space=pltpu.SMEM)


def sds(shape, dtype):
    return jax.ShapeDtypeStruct(shape, dtype)


def params(cid):
    return pltpu.CompilerParams(collective_id=cid, has_side_effects=True, vmem_limit_bytes=60 << 20)


def enc_forward(dp, gather, res, x, gains, shifts, proj, shards, de, dd):
    rows, width = x.shape[1:]
    total = 4 * rows
    slots = (4, rows, width)
    outs = []
    if gather:
        outs += [sds((de, shards[i].shape[1]), bf) for i in range(3)]
    outs += [sds((2, dd, shards[i].shape[1]), bf) for i in range(3, 6)]
    wide = shards[1].shape[1]
    outs += [
        sds(slots, bf),
        sds(slots, bf),
        sds((total, width), bf),
        sds((total, 256), bf),
        sds((total, wide), bf),
        sds((total, wide), bf),
        sds((rows, width), f32),
        sds((rows, width), bf),
        sds((4, rows, dd), bf),
    ]
    got = pl.pallas_call(
        functools.partial(enc_forward_kernel, dp, gather),
        out_shape=outs,
        in_specs=[SMEM] + vm(10),
        out_specs=vm(len(outs)),
        scratch_shapes=[
            pltpu.SemaphoreType.DMA((80,)),
            pltpu.SemaphoreType.DMA((80,)),
            pltpu.VMEM(slots, f32),
            pltpu.VMEM((2, 3, rows, width), bf),
            pltpu.VMEM((2, 3, rows, width), bf),
        ],
        compiler_params=params(1),
        name="enc_forward",
    )(res, x, gains, shifts, proj, *shards)
    if not gather:
        got = list(shards[:3]) + list(got)
    return got[:6], got[6:]


def dec_kernel(dp, *refs):
    it = iter(refs)
    take = lambda n: [next(it) for _ in range(n)]
    res, chosen_row, chosen_col, low_all, table, cot, gains, shifts, token, wd, we, wf = take(12)
    out, glow, gd, ge, gf, small = take(6)
    ss, rs = take(2)
    (n1, n2, gm, gmid_low, qg, kg, vg, gg, vtx, kt, ct, dqt, lse, acc_s, top_s, ctx, active, slope) = take(18)
    (dkv, mid_s, start_s, res_s, part, stage, recv, fstage, frecv, far, prod, pstage, precv, masks) = take(14)
    cx = Ctx(ss, rs, dp)
    cx.barrier([cx.core, cx.y, cx.x])
    rows, width = n1.shape[1:]
    m, lo, hi, s = cx.m, cx.lo, cx.hi, cx.s
    big = res[s] == 1
    shown = jnp.where(big, VIS, VIS_SMALL)
    filled = jnp.where(big, PATCHES, SMALL_PATCHES)
    pos_col = iota((rows, 1), 0) + m * rows
    live = jnp.where(pos_col < filled, 1.0, 0.0)
    gm[lo] = (cot[s].astype(f32) * live).astype(bf)
    cgm = cx.send(gm.at[lo], gm.at[lo], cx.core)
    vis = chosen_row.shape[-1]
    place = jnp.where((pos_col == chosen_row[s]) & (iota((1, vis), 1) < shown), 1.0, 0.0)
    seen = jnp.sum(place, axis=1, keepdims=True)
    weight = live - seen
    placed = nn(place.astype(bf), low_all[...].reshape(vis, width))
    half = width // 2
    nb, ns = rows // COLS_BIG, rows // COLS_SMALL
    rb = table[pl.ds(pl.multiple_of(m * nb, 8), nb), :]
    rsm = table[pl.ds(pl.multiple_of(m * ns, 8), ns), :]
    big_rows = jnp.broadcast_to(rb[:, None, :], (nb, COLS_BIG, half)).reshape(rows, half)
    small_rows = jnp.broadcast_to(rsm[:, None, :], (ns, COLS_SMALL, half)).reshape(rows, half)
    big_cols = jnp.broadcast_to(table[0:COLS_BIG, :][None], (nb, COLS_BIG, half)).reshape(rows, half)
    small_cols = jnp.broadcast_to(table[0:COLS_SMALL, :][None], (ns, COLS_SMALL, half)).reshape(rows, half)
    base = placed + weight * token[...]
    start_s[:, :half] = base[:, :half] + live * jnp.where(big, big_rows, small_rows)
    start_s[:, half:] = base[:, half:] + live * jnp.where(big, big_cols, small_cols)
    n1[m] = normalize(start_s[...], gains[0:1, :], shifts[0:1, :]).astype(bf)
    g1 = GatherMp(cx, n1)

    lane = iota((1, 256), 1)
    for j in range(4):
        head_lane = (lane < 128) & (lane // 32 == j)
        off = lane - (128 + 8 * j)
        masks[0, j] = jnp.where(head_lane | ((off >= 0) & (off < 3)) | (lane == 160), 1.0, 0.0).astype(bf)
        masks[1, j] = jnp.where(head_lane | ((off >= 0) & (off < 2)), 1.0, 0.0).astype(bf)
    aug = iota((1, 128), 1)
    total = 4 * rows
    key_bias = jnp.where(iota((total, 1), 0) < filled, 0.0, NEG)
    kaug = jnp.where(aug == 32, key_bias, jnp.where(aug < 32, 1.0, 0.0)).astype(bf)
    vaug = jnp.broadcast_to(jnp.where(aug < 32, 1.0, 0.0), (total, 128)).astype(bf)
    qaug = jnp.broadcast_to(jnp.where(aug == 32, 1.0, 0.0), (2 * rows, 128)).astype(bf)
    for g in range(2):
        kg[g, :, 128:] = kaug
        vg[g, :, 128:] = vaug
        qg[g, :, 128:] = qaug
    vtx[:, 32:, :] = jnp.ones((8, 16, total), bf)
    lse[...] = jnp.zeros_like(lse)

    def keys_values(i):
        at = pl.ds(pl.multiple_of(i * rows, 128), rows)
        for g in range(2):
            kv = nn(n1[i], wd[g, :, 128:384])
            kg[g, at, :128] = kv[:, :128].astype(bf)
            vg[g, at, :128] = kv[:, 128:].astype(bf)
            kvt = kv.T.astype(bf)
            for j in range(4):
                kt[4 * g + j, :, at] = kvt[32 * j : 32 * j + 32]
                vtx[4 * g + j, 0:32, at] = kvt[128 + 32 * j : 160 + 32 * j]

    g1.near()
    for r in range(2):
        for g in range(2):
            qg[g, r * rows : (r + 1) * rows, :128] = nn(n1[2 * hi + r], wd[g, :, :128]).astype(bf)
    keys_values(cx.m)
    keys_values(cx.m1)
    c2 = HD_DEC**-0.5 * LOG2E

    def head_pass(first, last, blocks):
        def body(h, _):
            g, j = h // 4, lax.rem(h, 4)
            if first:
                top, acc = None, None
            else:
                top, acc = top_s[h], acc_s[h]
            for i in blocks:
                at = pl.ds(pl.multiple_of(i * rows, 128), rows)
                sc = nt(kg[g, at, :] * masks[0, j], qg[g])
                mj = jnp.max(sc, axis=0, keepdims=True)
                new = mj if top is None else jnp.maximum(top, mj)
                p = jnp.exp2((sc - new) * c2).astype(bf)
                o = nn(vtx[h, :, at], p)
                acc = o if acc is None else acc * jnp.exp2((top - new) * c2) + o
                top = new
            if last:
                tot = acc[32:33, :]
                ct[h] = acc[:32, :] / tot
                at = pl.ds(pl.multiple_of(8 * j, 8), 8)
                lse[g, at, :] = jnp.broadcast_to(top + jnp.log(tot) * (LOG2E / c2), (8, top.shape[1]))
            else:
                top_s[h] = top
                acc_s[h] = acc
            return 0

        lax.fori_loop(0, 8, body, 0)

    head_pass(True, False, (cx.m, cx.m1))
    g1.forward()
    keys_values(cx.m2)
    g1.far()
    keys_values(cx.m3)
    head_pass(False, True, (cx.m2, cx.m3))
    for g in range(2):
        ctx[:, 128 * g : 128 * g + 128] = ct[4 * g : 4 * g + 4].reshape(128, 2 * rows).T.astype(bf)

    def reduce_core(slot, compute):
        fstage[slot] = compute(1 - lo).astype(bf)
        c = cx.send(fstage.at[slot], frecv.at[slot], cx.core)
        own = compute(lo)
        c.wait_recv()
        return own + frecv[slot].astype(f32)

    def chip_rows(r):
        return pl.ds(pl.multiple_of(r * rows, 128), rows)

    def out_rows(r):
        return sum(nt(ctx[chip_rows(r), 128 * g : 128 * g + 128], wd[g, :, 384:]) for g in range(2))

    mid = start_s[...] + reduce_core(0, out_rows)
    mid_s[...] = mid
    n2[lo] = normalize(mid, gains[1:2, :], shifts[1:2, :]).astype(bf)
    cn2 = cx.send(n2.at[lo], n2.at[lo], cx.core)

    def mlp_rows(r):
        at = chip_rows(r)
        x = n2[r]
        y = None
        for g in range(2):
            a, b = gelu_and_slope(nn(x, we[g]))
            cols = slice(width * g, width * (g + 1))
            a = a.astype(bf)
            active[at, cols] = a
            slope[at, cols] = b.astype(bf)
            t = nt(a, wf[g])
            y = t if y is None else y + t
        return y

    res_s[...] = mlp_rows(lo)
    cn2.wait_recv()
    fstage[1] = mlp_rows(1 - lo).astype(bf)
    c = cx.send(fstage.at[1], frecv.at[1], cx.core)

    cgm.wait_recv()

    def mlp_back_rows(r):
        at = chip_rows(r)
        y = None
        for g in range(2):
            cols = slice(width * g, width * (g + 1))
            ga = nn(gm[r], wf[g])
            gh = (ga * slope[at, cols].astype(f32)).astype(bf)
            slope[at, cols] = gh
            t = nt(gh, we[g])
            y = t if y is None else y + t
        return y

    fstage[2] = mlp_back_rows(1 - lo).astype(bf)
    cb = cx.send(fstage.at[2], frecv.at[2], cx.core)
    c.wait_recv()
    result = mid_s[...] + res_s[...] + frecv[1].astype(f32)
    produced = (result * live).astype(bf)
    prod[0] = produced[:, :half]
    prod[1] = produced[:, half:]
    out[s] = prod[s]
    cprod = cx.send(prod.at[1 - s], out.at[s], cx.x)
    own = mlp_back_rows(lo)
    gm_all = gm[...].reshape(2 * rows, width)
    for g in range(2):
        cols = slice(width * g, width * (g + 1))
        gf[g] = tn(gm_all, active[:, cols])
    cb.wait_recv()
    grad_mid, gain_mid, shift_mid = normalize_back(mid_s[...], gains[1:2, :], own + frecv[2].astype(f32))
    gmid = gm[lo].astype(f32) + grad_mid
    mid_s[...] = gmid
    gmid_low[lo] = gmid.astype(bf)
    cgmid = cx.send(gmid_low.at[lo], gmid_low.at[lo], cx.core)
    n2_all = n2[...].reshape(2 * rows, width)
    for g in range(2):
        cols = slice(width * g, width * (g + 1))
        ge[g] = tn(n2_all, slope[:, cols])
    cgmid.wait_recv()
    gmid_all = gmid_low[...].reshape(2 * rows, width)
    sel = jnp.where(iota((128, 128), 0) // 32 == iota((128, 128), 1) // 8, 1.0, 0.0).astype(bf)
    lane128 = iota((1, 128), 1)
    t8 = lax.rem(lane128, 8)
    for g in range(2):
        gcg = nn(gmid_all, wd[g, :, 384:]).astype(bf)
        gg[g, :, :128] = gcg
        prodd = gcg.astype(f32) * ctx[:, 128 * g : 128 * g + 128].astype(f32)
        ph = prodd.astype(bf)
        plow = (prodd - ph.astype(f32)).astype(bf)
        delta = nn(ph, sel) + nn(plow, sel)
        dh = delta.astype(bf).astype(f32)
        daug = jnp.where(t8 == 0, -dh, jnp.where(t8 == 1, dh - delta, 0.0))
        gg[g, :, 128:] = jnp.where(lane128 < 32, daug, 0.0).astype(bf)
        gd[g, :, 384:] = tn(gmid_all, ctx[:, 128 * g : 128 * g + 128])
        lt = lse[g].T
        h1 = lt.astype(bf).astype(f32)
        h2 = (lt - h1).astype(bf).astype(f32)
        h3 = lt - h1 - h2
        laug = jnp.where(t8 == 0, -h1, jnp.where(t8 == 1, -h2, jnp.where(t8 == 2, -h3, 0.0)))
        laug = jnp.where(lane128 == 32, 1.0, jnp.where(lane128 < 32, laug, 0.0))
        qg[g, :, 128:] = laug.astype(bf)

    scale = HD_DEC**-0.5
    dqt[...] = jnp.zeros_like(dqt)
    head_lane = lane128 // 32

    def back_pass(blocks):
        def body(h, _):
            g, j = h // 4, lax.rem(h, 4)
            mine = head_lane == j
            for i in blocks:
                at = pl.ds(pl.multiple_of(i * rows, 128), rows)
                st = nt(kg[g, at, :] * masks[0, j], qg[g])
                dpt = nt(vg[g, at, :] * masks[1, j], gg[g])
                p = jnp.exp2(st * c2)
                ds = (p * dpt).astype(bf)
                dv = nn(p.astype(bf), gg[g, :, :128])
                dk = nn(ds, qg[g, :, :128]) * scale
                dkv[g, at, :128] = jnp.where(mine, dk, dkv[g, at, :128].astype(f32)).astype(bf)
                dkv[g, at, 128:] = jnp.where(mine, dv, dkv[g, at, 128:].astype(f32)).astype(bf)
                dqt[h] += nn(kt[h, :, at], ds)
            return 0

        lax.fori_loop(0, 8, body, 0)

    dkv[...] = jnp.zeros_like(dkv)
    back_pass((cx.m2, cx.m3))

    def far_rows(r):
        at = pl.ds(pl.multiple_of((2 * (1 - hi) + r) * rows, 128), rows)
        return sum(nt(dkv[g, at, :], wd[g, :, 128:384]) for g in range(2))

    far[0] = reduce_core(3, far_rows).astype(bf)
    cfar = cx.send(far.at[0], far.at[1], cx.y)
    back_pass((cx.m, cx.m1))
    for g in range(2):
        ctx[:, 128 * g : 128 * g + 128] = (dqt[4 * g : 4 * g + 4].reshape(128, 2 * rows).T * scale).astype(bf)

    def near_rows(r):
        at = pl.ds(pl.multiple_of((2 * hi + r) * rows, 128), rows)
        return sum(
            nt(ctx[chip_rows(r), 128 * g : 128 * g + 128], wd[g, :, :128]) + nt(dkv[g, at, :], wd[g, :, 128:384])
            for g in range(2)
        )

    near = reduce_core(4, near_rows)
    cfar.wait_recv()
    grad_in, gain_in, shift_in = normalize_back(start_s[...], gains[0:1, :], near + far[1].astype(f32))
    gstart = (mid_s[...] + grad_in).astype(bf)
    token_term = jnp.sum(weight * gstart.astype(f32), axis=0, keepdims=True)
    small[0:1] = gain_in
    small[1:2] = gain_mid
    small[2:3] = shift_in
    small[3:4] = shift_mid
    small[4:5] = token_term
    small[5:8] = jnp.zeros((3, width), f32)
    pos_row = iota((1, rows), 1) + m * rows
    place_t = jnp.where((chosen_col[s] == pos_row) & (iota((vis, 1), 0) < shown), 1.0, 0.0).astype(bf)
    part[...] = nn(place_t, gstart).reshape(part.shape)
    n1_chip = n1[pl.ds(2 * hi, 2)].reshape(2 * rows, width)
    for g in range(2):
        gd[g, :, :128] = tn(n1_chip, ctx[:, 128 * g : 128 * g + 128])
        gd[g, :, 128:384] = tn(n1[...].reshape(total, width), dkv[g])
    glow[...] = reduce_mp(cx, part, pstage, precv).astype(bf)
    cprod.wait_recv()
    cx.drain()


def decoder(dp, res, chosen_row, chosen_col, low_all, table, cot, gains, shifts, token, wd, we, wf):
    rows, width = cot.shape[1:]
    vis = chosen_row.shape[-1]
    total, chip = 4 * rows, 2 * rows
    outs = [
        sds((2, rows, width // 2), bf),
        sds((vis // 4, width), bf),
        sds(wd.shape, f32),
        sds(we.shape, f32),
        sds(wf.shape, f32),
        sds((8, width), f32),
    ]
    V = pltpu.VMEM
    return pl.pallas_call(
        functools.partial(dec_kernel, dp),
        out_shape=outs,
        in_specs=[SMEM] + vm(11),
        out_specs=vm(len(outs)),
        scratch_shapes=[
            pltpu.SemaphoreType.DMA((32,)),
            pltpu.SemaphoreType.DMA((32,)),
            V((4, rows, width), bf),
            V((2, rows, width), bf),
            V((2, rows, width), bf),
            V((2, rows, width), bf),
            V((2, chip, 256), bf),
            V((2, total, 256), bf),
            V((2, total, 256), bf),
            V((2, chip, 256), bf),
            V((8, 48, total), bf),
            V((8, 32, total), bf),
            V((8, 32, chip), f32),
            V((8, 32, chip), f32),
            V((2, 128, chip), f32),
            V((8, 48, chip), f32),
            V((8, 1, chip), f32),
            V((chip, 256), bf),
            V((chip, 2 * width), bf),
            V((chip, 2 * width), bf),
            V((2, total, 256), bf),
            V((rows, width), f32),
            V((rows, width), f32),
            V((rows, width), f32),
            V((4, vis // 4, width), f32),
            V((1,), f32) if False else V((8, 128), f32),
            V((8, 128), f32),
            V((5, rows, width), bf),
            V((5, rows, width), bf),
            V((2, rows, width), bf),
            V((2, rows, width // 2), bf),
            V((3, vis // 4, width), bf),
            V((3, vis // 4, width), bf),
            V((2, 4, 1, 256), bf),
        ],
        compiler_params=params(2),
        name="decoder",
    )(res, chosen_row, chosen_col, low_all, table, cot, gains, shifts, token, wd, we, wf)


def enc_backward_kernel(dp, gather, *refs):
    it = iter(refs)
    take = lambda n: [next(it) for _ in range(n)]
    res, x_all, gains, proj, wa, wb, wc, n1, n2, qkv, ctx, slope, active, mid, top, glow, dd, de, df, dsmall = take(20)
    gin, out_a, out_b, out_c, out_d, out_e, out_f, small, pout = take(9)
    ss, rs, gm, gmid_low, gqkv, part, stage, recv, gbuf, yst, yrc = take(11)
    if gather:
        exs, exr, ezs, ezr, dxs, dxr, dzs, dzr, ga, gb, gc, smr, smz, pst, prc, pz, pacc = take(17)
    else:
        (gmid_half,) = take(1)
        ga, gb, gc = out_a, out_b, out_c
    if gather:
        (gmid_half,) = take(1)
    cx = Ctx(ss, rs, dp)
    peers = [cx.core, cx.y, cx.x]
    if gather:
        peers += [cx.z(k) for k in range(1, dp)]
    cx.barrier(peers)
    m, s = cx.m, cx.s
    rows, width = n1.shape[1:]
    total = 4 * rows
    g_top = nt(glow[...], proj[...])
    gm[m] = g_top.astype(bf)
    g1 = GatherMp(cx, gm)
    ys = []
    for i, src in enumerate((df, de, dd)):
        yst[i] = src[1].astype(bf)
        ys.append(cx.send(yst.at[i], yrc.at[i], cx.y))
    g1.finish()
    gm_all = gm[...].reshape(total, width)
    gact = nn(gm_all, wc[...])
    gh = (gact * slope[...].astype(f32)).astype(bf)
    part[...] = nt(gh, wb[...]).reshape(part.shape)
    gb[...] = tn(n2[...].reshape(total, width), gh)
    gc[...] = tn(gm_all, active[...])
    g_n2 = reduce_mp(cx, part, stage.at[0], recv.at[0])
    grad_mid, gain_mid, shift_mid = normalize_back(mid[...], gains[1:2, :], g_n2)
    gmid = g_top + grad_mid
    gmid_half[...] = gmid
    gmid_low[m] = gmid.astype(bf)
    g2 = GatherMp(cx, gmid_low)
    sc = []
    if gather:
        er, dr = x_rows(wa, dp), x_rows(wd_shape(dd), dp)
        sb = ScatterW(cx, er, out_b, exs.at[0], exr.at[0], ezs.at[0], ezr.at[0])
        sb.start(gb)
        scc = ScatterW(cx, er, out_c, exs.at[1], exr.at[1], ezs.at[1], ezr.at[1])
        scc.start(gc)
    dsum = []
    for i, src in enumerate((df, de, dd)):
        ys[i].wait_recv()
        gbuf[i] = src[0] + yrc[i].astype(f32)
        if gather:
            o = (out_f, out_e, out_d)[i]
            q = ScatterW(cx, dr, o, dxs.at[i], dxr.at[i], dzs.at[i], dzr.at[i])
            q.start(gbuf.at[i])
            dsum.append(q)
        else:
            (out_f, out_e, out_d)[i][...] = gbuf[i]
    p_part = tn(top[...], glow[...])
    if gather:
        pr = ProjSum(cx, pst, prc, pz, pacc, pout)
        pr.core(p_part)
    else:
        pout[...] = p_part
    g2.finish()
    gmid_all = gmid_low[...].reshape(total, width)
    cpad = ctx.shape[1]
    gcx = nn(gmid_all, wa[:, width - cpad :]).astype(bf)
    shown = jnp.where(res[s] == 1, VIS, VIS_SMALL)
    bias = jnp.where(iota((1, total), 1) < shown, 0.0, NEG)
    scale = HD_ENC**-0.5
    scale2 = scale * LOG2E
    heads = (width // 4) // HD_ENC
    for h in range(heads):
        q = qkv[:, h * HD_ENC : (h + 1) * HD_ENC]
        k = qkv[:, (heads + h) * HD_ENC : (heads + h + 1) * HD_ENC]
        v = qkv[:, (2 * heads + h) * HD_ENC : (2 * heads + h + 1) * HD_ENC]
        go = gcx[:, (h + 1) * HD_ENC : (h + 2) * HD_ENC]
        co = ctx[:, (h + 1) * HD_ENC : (h + 2) * HD_ENC]
        scr = nt(q, k) + bias
        e = jnp.exp2((scr - jnp.max(scr, axis=1, keepdims=True)) * scale2)
        p = e / jnp.sum(e, axis=1, keepdims=True)
        delta = jnp.sum(go.astype(f32) * co.astype(f32), axis=1, keepdims=True)
        gs = (p * (nt(go, v) - delta) * scale).astype(bf)
        gqkv[:, h * HD_ENC : (h + 1) * HD_ENC] = nn(gs, k).astype(bf)
        gqkv[:, (heads + h) * HD_ENC : (heads + h + 1) * HD_ENC] = tn(gs, q).astype(bf)
        gqkv[:, (2 * heads + h) * HD_ENC : (2 * heads + h + 1) * HD_ENC] = tn(p.astype(bf), go).astype(bf)
        if gather and h == 0:
            sb.middle()
            pr.y()
        if gather and h == 1:
            scc.middle()
    gqkv[:, 3 * heads * HD_ENC :] = jnp.zeros((total, width - 3 * heads * HD_ENC), bf)
    part[...] = nt(gqkv[...], wa[...]).reshape(part.shape)
    n1_all = n1[...].reshape(total, width)
    cut = width - cpad
    ga[:, :cut] = tn(n1_all, gqkv[:, :cut])
    ga[:, cut:] = tn(n1_all, gqkv[:, cut:]) + tn(gmid_all, ctx[...])
    if gather:
        sa = ScatterW(cx, er, out_a, exs.at[2], exr.at[2], ezs.at[2], ezr.at[2])
        sa.start(ga)
    g_n1 = reduce_mp(cx, part, stage.at[1], recv.at[1])
    stream = x_all[s].astype(f32)
    grad_in, gain_in, shift_in = normalize_back(stream, gains[0:1, :], g_n1)
    grad = gmid_half[...] + grad_in
    half = width // 2
    part[0, :, :half] = grad[:, :half]
    part[1, :, :half] = grad[:, half:]
    gin[s] = part[s, :, :half]
    cin = cx.send(part.at[1 - s, :, pl.ds(0, half)], gin.at[s], cx.x)
    dw = dsmall.shape[1]
    vec = jnp.concatenate(
        [
            gain_in,
            gain_mid,
            shift_in,
            shift_mid,
            jnp.zeros((4, width), f32),
            jnp.concatenate([dsmall[...], jnp.zeros((8, width - dw), f32)], axis=1),
        ],
        axis=0,
    )
    if gather:
        smr[0] = vec
        c = cx.send(smr.at[0], smr.at[1], cx.core)
        pr.x()
        for q in dsum:
            q.middle()
        c.wait_recv()
        smr[2] = smr[0] + smr[1]
        c = cx.send(smr.at[2], smr.at[3], cx.y)
        sa.middle()
        c.wait_recv()
        smr[4] = smr[2] + smr[3]
        c = cx.send(smr.at[4], smr.at[5], cx.x)
        pr.z()
        c.wait_recv()
        smz[cx.d] = smr[4] + smr[5]
        cs = [cx.send(smz.at[cx.d], smz.at[cx.d], cx.z(k)) for k in range(1, dp)]
        pr.back_x()
        sb.finish()
        scc.finish()
        pr.back_y()
        for q in dsum:
            q.finish()
        for c in cs:
            c.wait_recv()
        small[...] = sum_in_order(smz, dp)
        pr.back_core()
        sa.finish()
        pr.finish()
    else:
        small[...] = vec
    cin.wait_recv()
    cx.drain()


def sum_in_order(ref, n):
    out = ref[0]
    for i in range(1, n):
        out = out + ref[i]
    return out


def x_rows(w, dp):
    return w.shape[0] // (2 * dp)


class wd_shape:
    def __init__(self, ref):
        self.shape = ref.shape[1:]


class ProjSum:
    def __init__(self, cx, st, rc, zb, acc, out):
        self.cx, self.st, self.rc, self.zb, self.acc, self.out = cx, st, rc, zb, acc, out
        self.R = out.shape[0]

    def rows(self, start, size):
        return pl.ds(pl.multiple_of(start, 16), size)

    def core(self, part):
        cx, R = self.cx, self.R
        h = R // 2
        self.acc[...] = part
        self.o1 = cx.lo * h
        self.st[0:h] = self.acc[self.rows((1 - cx.lo) * h, h), :].astype(bf)
        self.c = cx.send(self.st.at[pl.ds(0, h)], self.rc.at[pl.ds(0, h)], cx.core)

    def step(self, prev_at, prev_size, base, bit, dev):
        cx, R = self.cx, self.R
        self.c.wait_recv()
        off = R - 2 * prev_size
        mine = self.rows(prev_at, prev_size)
        self.acc[mine, :] = self.acc[mine, :] + self.rc[off : off + prev_size, :].astype(f32)
        h = prev_size // 2
        noff = R - 2 * h
        self.st[noff : noff + h] = self.acc[self.rows(prev_at + (1 - bit) * h, h), :].astype(bf)
        self.c = cx.send(self.st.at[pl.ds(noff, h)], self.rc.at[pl.ds(noff, h)], dev)
        return prev_at + bit * h

    def y(self):
        self.o2 = self.step(self.o1, self.R // 2, 0, self.cx.hi, self.cx.y)

    def x(self):
        self.o3 = self.step(self.o2, self.R // 4, 0, self.cx.s, self.cx.x)

    def z(self):
        cx, R = self.cx, self.R
        size = R // 8
        self.c.wait_recv()
        off = R - 2 * size
        self.zb[cx.d] = self.acc[self.rows(self.o3, size), :] + self.rc[off : off + size, :].astype(f32)
        self.cs = [cx.send(self.zb.at[cx.d], self.zb.at[cx.d], cx.z(k)) for k in range(1, cx.dp)]

    def back_x(self):
        cx, R = self.cx, self.R
        for c in self.cs:
            c.wait_recv()
        at = self.rows(self.o3, R // 8)
        self.out[at, :] = sum_in_order(self.zb, cx.dp)
        self.c = cx.send(self.out.at[at], self.out.at[at], cx.x)

    def back_y(self):
        self.c.wait_recv()
        at = self.rows(self.o2, self.R // 4)
        self.c = self.cx.send(self.out.at[at], self.out.at[at], self.cx.y)

    def back_core(self):
        self.c.wait_recv()
        at = self.rows(self.o1, self.R // 2)
        self.c = self.cx.send(self.out.at[at], self.out.at[at], self.cx.core)

    def finish(self):
        self.c.wait_recv()


def enc_backward(dp, gather, res, x, gains, proj, weights, saved, glow, dgrads, dsmall):
    wa, wb, wc = weights
    n1, n2, qkv, ctx, slope, active, mid, top = saved
    rows, width = x.shape[1:]
    total = 4 * rows
    V = pltpu.VMEM
    dd = dgrads[0].shape
    if gather:
        er, dr = wa.shape[0] // (2 * dp), dd[1] // (2 * dp)
    else:
        er, dr = wa.shape[0], dd[1]
    outs = [sds((2, rows, width // 2), f32)]
    outs += [sds((er, w.shape[1]), f32) for w in weights]
    outs += [sds((dr, dd[2]), f32)] * 3
    outs += [sds((16, width), f32), sds(proj.shape, f32)]
    slots = (4, rows, width)
    scratch = [
        pltpu.SemaphoreType.DMA((96,)),
        pltpu.SemaphoreType.DMA((96,)),
        V(slots, bf),
        V(slots, bf),
        V((total, width), bf),
        V(slots, f32),
        V((2, 3, rows, width), bf),
        V((2, 3, rows, width), bf),
        V((3,) + dd[1:], f32),
        V((3,) + dd[1:], bf),
        V((3,) + dd[1:], bf),
    ]
    if gather:
        cols = wa.shape[1]
        scratch += [
            V((3, dp * er, cols), bf),
            V((3, dp * er, cols), bf),
            V((3, dp * er, cols), bf),
            V((3, dp - 1, er, cols), bf),
            V((3, dp * dr, dd[2]), bf),
            V((3, dp * dr, dd[2]), bf),
            V((3, dp * dr, dd[2]), bf),
            V((3, dp - 1, dr, dd[2]), bf),
            V(wa.shape, f32),
            V(wb.shape, f32),
            V(wc.shape, f32),
            V((6, 16, width), f32),
            V((dp, 16, width), f32),
            V(proj.shape, bf),
            V(proj.shape, bf),
            V((dp, proj.shape[0] // 8, proj.shape[1]), f32),
            V(proj.shape, f32),
        ]
    scratch += [V((rows, width), f32)]
    return pl.pallas_call(
        functools.partial(enc_backward_kernel, dp, gather),
        out_shape=outs,
        in_specs=[SMEM] + vm(19),
        out_specs=vm(len(outs)),
        scratch_shapes=scratch,
        compiler_params=params(3),
        name="enc_backward",
    )(res, x, gains, proj, wa, wb, wc, n1, n2, qkv, ctx, slope, active, mid, top, glow, *dgrads, dsmall)


def position_table(count, quarter):
    freq = (np.float32(10000.0) ** (-np.arange(quarter, dtype=np.float32) / np.float32(quarter))).astype(np.float32)
    angle = (np.arange(count, dtype=np.float32)[:, None] * freq[None, :]).astype(np.float32).astype(np.float64)
    return np.concatenate([np.sin(angle), np.cos(angle)], axis=1).astype(np.float32)


def per_device(
    x_visible,
    resolution,
    visible_index,
    enc_qkv_w,
    enc_out_w,
    enc_up_w,
    enc_down_w,
    enc_gains,
    enc_shifts,
    projection,
    mask_token,
    dec_qkv_w,
    dec_out_w,
    dec_up_w,
    dec_down_w,
    dec_gains,
    dec_shifts,
    cotangent,
):
    dp = lax.axis_size("dp")
    over = ("section", "dp")
    er, dr = enc_qkv_w.shape[0], dec_qkv_w.shape[0]
    de, dd = projection.shape
    ec, dc = enc_qkv_w.shape[2], dec_qkv_w.shape[2]
    gather = er % 16 == 0 and dr % 16 == 0
    shards = [
        jnp.concatenate([enc_qkv_w.reshape(er, 3 * ec), enc_out_w.T], axis=1),
        enc_up_w,
        enc_down_w.T,
        jnp.concatenate([dec_qkv_w.reshape(dr, 3 * dc), dec_out_w.T], axis=1),
        dec_up_w,
        dec_down_w.T,
    ]
    if not gather:
        shards = [lax.all_gather(w, over, axis=0, tiled=True) for w in shards]
    weights, saved = enc_forward(
        dp, gather, resolution, x_visible, enc_gains, enc_shifts, projection, shards, de, dd
    )
    table = jnp.asarray(position_table(COLS_BIG, dd // 4))
    out, glow, gd, ge, gf, dsmall = decoder(
        dp,
        resolution,
        visible_index[:, None, :],
        visible_index[:, :, None],
        saved[8],
        table,
        cotangent,
        dec_gains,
        dec_shifts,
        mask_token[None, :],
        *weights[3:],
    )
    gin, ga, gb, gc, hd, he, hf, small, pgrad = enc_backward(
        dp,
        gather,
        resolution,
        x_visible,
        enc_gains,
        projection,
        weights[:3],
        saved[:8],
        glow,
        (gd, ge, gf),
        dsmall,
    )
    if not gather:
        ga, gb, gc, hd, he, hf = [
            lax.psum_scatter(g, over, scatter_dimension=0, tiled=True) for g in (ga, gb, gc, hd, he, hf)
        ]
        small, pgrad = lax.psum((small, pgrad), ("section", "dp", "mp"))
    return (
        out,
        gin,
        ga[:, : 3 * ec].reshape(er, 3, ec),
        ga[:, 3 * ec :].T,
        gb,
        gc.T,
        small[0:2],
        small[2:4],
        pgrad,
        small[12, :dd],
        hd[:, : 3 * dc].reshape(dr, 3, dc),
        hd[:, 3 * dc :].T,
        he,
        hf.T,
        small[8:10, :dd],
        small[10:12, :dd],
    )


def solution(mesh):
    matrix_in = P(("section", "dp"), "mp")
    matrix_out = P("mp", ("section", "dp"))
    qkv = P(("section", "dp"), None, "mp")
    return jax.shard_map(
        per_device,
        mesh=mesh,
        in_specs=(
            P("dp", "mp", None),
            P("dp"),
            P("dp", None),
            qkv,
            matrix_out,
            matrix_in,
            matrix_out,
            P(),
            P(),
            P(),
            P(),
            qkv,
            matrix_out,
            matrix_in,
            matrix_out,
            P(),
            P(),
            P("dp", "mp", None),
        ),
        out_specs=(
            P("dp", "mp", "section"),
            P("dp", "mp", "section"),
            qkv,
            matrix_out,
            matrix_in,
            matrix_out,
            P(),
            P(),
            P(),
            P(),
            qkv,
            matrix_out,
            matrix_in,
            matrix_out,
            P(),
            P(),
        ),
        check_vma=False,
    )
```

time: 2790 us -> 443 us (0.16)
  waiting for transfers between devices: 1360 us -> 0 us
  matrix products: 817 us -> 0 us
  Pallas kernels: 0 us -> 414 us
  blocking collectives: 323 us -> 0 us
  other arithmetic: 99.9 us -> 2.11 us
  local copies, waits for them, and re-layouts: 98.7 us -> 21.4 us
  loops' own time: 42.6 us -> 0 us
    reduce_scatter x25 -> x0, waiting for transfers between devices: 1020 us -> none  [the longest x16 495 us: spread(): lax.psum_scatter(jnp.dot(left_rows, weight, preferred_element_type=jnp.fl...]
    dot_general x120 -> x0, matrix products: 810 us -> none  [the longest x10 256 us: one_block(): jnp.einsum('hqk,khd->qhd', grad_raw, key_rows, preferred_element_type=jnp...]
    pallas_call x0 -> x3, Pallas kernels: none -> 414 us  [the longest x1 162 us: enc_backward(): pl.pallas_call(functools.partial(enc_backward_kernel, dp, gather), out_sh...]
    all_gather x16 -> x0, blocking collectives: 282 us -> none  [the longest x8 64.3 us: collect(): return lax.all_gather(rows_low, 'mp', axis=0, tiled=True)]
    all_gather x10 -> x0, waiting for transfers between devices: 155 us -> none  [the longest x8 155 us: collect(): return lax.all_gather(rows_low, 'mp', axis=0, tiled=True)]
    psum x1 -> x0, waiting for transfers between devices: 138 us -> none  [per_device(): lax.psum((enc_acc[4], enc_acc[5], enc_acc[6], dec_acc[6], dec_acc[4], dec...]
    reduce_sum x36 -> x0, other arithmetic: 57.9 us -> none  [the longest x10 30.9 us: one_block(): totals = jnp.sum(weights, axis=-1, keepdims=True)]
    while x558 -> x0, local copies, waits for them, and re-layouts: 51.2 us -> none
  transfers between devices with their start and end apart: 45 -> 0, of which waited for: 43 -> 0; matrix products, arithmetic and copies ran while one was open for 4% -> 0% of each run, Pallas kernels for 0% -> 0%
where the time goes in v1:
time: 443 us; the launch traced here: 438 us
  Pallas kernels  414 us (93%)
  local copies, waits for them, and re-layouts  21.4 us (5%)
    pallas_call x1, Pallas kernels, enc_backward(): pl.pallas_call(functools.partial(enc_backward_kernel, dp, gather), out_sh...  162 us
    pallas_call x1, Pallas kernels, decoder(): pl.pallas_call(functools.partial(dec_kernel, dp), out_shape=outs, in_spec...  131 us
    pallas_call x1, Pallas kernels, enc_forward(): pl.pallas_call(functools.partial(enc_forward_kernel, dp, gather), out_sha...  121 us
    unnamed x28, local copies, waits for them, and re-layouts  10.6 us

profile of v1, /device:TPU:0, one launch (start us, length us, event | category | flops | bytes accessed | tf_op | source)
XLA Modules:
  0.0 438.3 jit_solution(6625451393008805352)
XLA Ops:
  0.6 0.0 copy-start
  0.7 1.3 broadcast_in_dim.9.refs_1_
  2.0 0.9 copy.42
  2.8 0.0 copy-done
  2.9 1.4 pad_maximum_fusion.1.refs_8_
  4.2 1.1 copy.41
  5.3 0.2 copy.43
  5.5 0.8 pad_maximum_fusion.refs_5_
  6.2 1.7 copy.45.refs_2_
  7.9 121.1 %enc_forward.1 = (bf16[768,768]{1,0:T(8,128)(2,1)}, bf16[768,768]{1,0:T(8,128)(2,1)}, bf16[768,768]{1,0:T(8,128)(2,1)}, bf16[2,512,512]{2,1,0:T(8,128)(2,1)}, bf...) custom-call(s32[2]{0:T(128)} %refs_0_.5, ...), custom_call_target="tpu_custom_call" | custom-call | tf_op jit(solution)/shard_map/enc_forward/pallas_call | solution.py:360
  129.0 131.1 %decoder.1 = (bf16[2,512,256]{2,1,0:T(8,128)(2,1)}, bf16[128,512]{1,0:T(8,128)(2,1)}, f32[2,512,512]{2,1,0:T(8,128)}, f32[2,512,512]{2,1,0:T(8,128)}, f32[2,512,512]{2,1,0:T(8,128)}, /*index=5*/f32[8,512]{1,0:T(8,128)}) custom-call(s32[2]{0:T(128)} %refs_0_.5, s32[2,1,512]{2,1,0:T(1,128)} %broadcast_in_dim.9.refs_1_, s32[2,512,1]{2,1,0:T(8,128)} %copy.45.refs_2_, ...), custom_call_target="tpu_custom_call" | custom-call | tf_op jit(solution)/shard_map/decoder/pallas_call | solution.py:671
  260.1 161.6 %enc_backward.1 = (f32[2,128,384]{2,1,0:T(8,128)}, f32[96,768]{1,0:T(8,128)}, f32[96,768]{1,0:T(8,128)}, f32[96,768]{1,0:T(8,128)}, f32[64,512]{1,0:T(8,128)}, /...) custom-call(s32[2]{0:T(128)} %refs_0_.5, bf16[2,128,768]{2,1,0:T(8,128)(2,1)} %refs_1_.3, ...), custom_call_target="tpu_custom_call" | custom-call | tf_op jit(solution)/shard_map/enc_backward/pallas_call | solution.py:1006
  421.7 0.0 copy-start.2
  421.7 1.4 slice.31
  423.1 1.4 fusion
  424.5 1.4 fusion.1
  425.9 1.4 slice_bitcast_fusion.2
  427.3 1.5 copy_bitcast_fusion
  428.8 0.0 copy-start.3
  428.8 1.0 slice_bitcast_fusion.1
  429.8 1.0 slice.27
  430.8 0.0 copy-start.5
  430.8 0.7 copy.48
  431.6 0.1 copy.46
  431.7 0.0 copy-start.4
  431.7 0.9 copy.47
  432.6 0.0 copy-done.2
  432.6 0.0 copy-start.1
  432.6 0.8 copy.61
  433.4 0.0 copy-done.3
  433.4 0.7 copy.62
  434.1 0.0 copy-done.5
  434.1 0.7 copy.63
  434.9 0.0 copy-done.4
  434.9 0.7 copy.64
  435.6 0.0 copy-done.1
  435.6 0.0 copy-start.7
  435.6 0.0 copy-start.6
  435.6 1.1 copy.65
  436.7 0.0 copy-done.7
  436.7 0.7 copy.66
  437.4 0.0 copy-done.6
  437.4 0.7 copy.67
  (1 shorter events, 0.0 us)
Async XLA Ops:
  0.6 2.2 copy-start
  421.7 10.9 %copy-start.2 = (bf16[2,512,256]{2,1,0:T(8,128)(2,1)S(1)}, bf16[2,512,256]{2,1,0:T(8,128)(2,1)}, u32[]{:S(2)}) copy-start(bf16[2,512,256]{2,1,0:T(8,128)(2,1)} %get-tuple-element.128) | copy-start | bytes 1572868
  428.8 4.6 %copy-start.3 = (f32[2,128,384]{2,1,0:T(8,128)S(1)}, f32[2,128,384]{2,1,0:T(8,128)}, u32[]{:S(2)}) copy-start(f32[2,128,384]{2,1,0:T(8,128)} %get-tuple-element.129) | copy-start | bytes 1179652
  430.8 3.3 copy-start.5
  431.7 3.2 copy-start.4
  432.6 3.0 copy-start.1
  435.6 1.1 copy-start.7
  435.6 1.8 copy-start.6
